TPU v7x, 128 devices: a whole 4x4x4 slice. The times are simulated.
128 devices in a mesh: ctx: 32 (over z, y, core), head: 4 (over x).
Axes of the slice: x: 4, y: 4, z: 4, core: 2. Of those that a mesh axis runs over, the one named last changes fastest.
Arguments:
- queries: bfloat16 [4096, 4096], P(('ctx', 'head')), may hold values from -7.2 to 7.2
- keys: bfloat16 [4096, 512], P(('ctx', 'head')), may hold values from -7.2 to 7.2
- values: bfloat16 [4096, 512], P(('ctx', 'head')), may hold values from -6 to 6
- grad_out: bfloat16 [4096, 4096], P('ctx', 'head'), may hold values from -6 to 6
- owner_lists: int32 [32, 2], replicated, may hold values from 0 to 63, as said below
- doc_lengths: int32 [16], replicated, may hold values from 1 to 2048, as said below
Outputs:
- attn_out: bfloat16 [4096, 4096], P('ctx', 'head')
- grad_q: bfloat16 [4096, 4096], P(('ctx', 'head'))
- grad_k: bfloat16 [4096, 512], P(('ctx', 'head'))
- grad_v: bfloat16 [4096, 512], P(('ctx', 'head'))
Inputs may be any that keep to these rules, and one draw needn't show every extreme that they name: `owner_lists`: row r names the two stretches of 64 positions that owner r receives; each of the 64 stretches is named exactly once. `doc_lengths`: lengths of the packed documents in order; they sum to 4096 and the longest is exactly 2048.
All inputs are finite; a program needn't handle non-finite values.
Results may differ from a plain program's by a relative error of at most 0.015.
Values may be sent and summed in bfloat16 or wider, within the bound.
A program may use at most 64 MiB of HBM per device.

v0:
```python
import functools
import math

import jax
import jax.numpy as jnp
from jax import lax
from jax.experimental import pallas as pl
from jax.experimental.pallas import tpu as pltpu
from jax.sharding import PartitionSpec as P

MESH = pl.DeviceIdType.MESH
BF16 = jnp.bfloat16
F32 = jnp.float32

N_CTX, N_HEAD = 32, 4
NZ, NY, NCORE = 4, 4, 2
PLANE = NY * NCORE
PLANES = 3
WINDOW = 17
TOK = 128
PART = 32
DIM = 128
GROUP = 8
ROWS = TOK * GROUP
COLS = GROUP * DIM
NDOCS = 16
MASKED = -1e30
SCALE = 1.0 / math.sqrt(DIM)
LOG2E = 1.0 / math.log(2.0)

XK, XV, XQ, G1, G2, A1, A2, DQ, DK, DV = range(10)
Z1, Z2, Y0, C0, CP, YP, ZP = 10, 11, 12, 15, 18, 21, 24
N_SEM = 26
LQ, LK, LV, LG, LA, LDQ, LDK, LDV = range(8)
N_LOCAL = 8


def body(
    q_in, k_in, v_in, go_in, slot_of, owned, doc_lengths,
    ao, gq, gk, gv,
    kv, qs, gcol, gperm, gos, acol, aperm, out_rows, dq_rows,
    q_rows, q_cols, go_cols, probs, parts, from_core, y_sum, from_y, z_sum, from_z, grads,
    send, recv, local,
):
    c = lax.axis_index("ctx")
    h = lax.axis_index("head")
    z = c // PLANE
    idx = lax.rem(c, PLANE)
    y = idx // NCORE
    co = lax.rem(idx, NCORE)
    sib = c + 1 - 2 * co
    tile_row = pl.multiple_of(16 * (c // GROUP), 16)
    tile_head = lax.rem(c, GROUP)

    def ctx_at(zz, yy):
        return lax.rem(zz, NZ) * PLANE + lax.rem(yy, NY) * NCORE + co

    def push(src, dst, sem, ctx, head):
        copy = pltpu.make_async_remote_copy(
            src_ref=src, dst_ref=dst, send_sem=send.at[sem], recv_sem=recv.at[sem],
            device_id=(ctx, head), device_id_type=MESH,
        )
        copy.start()

    def drain(ref, sem):
        pltpu.make_async_copy(ref, ref, sem).wait()

    def cols(number, width):
        return pl.ds(pl.multiple_of(number * width, width), width)

    local_copies = [
        pltpu.make_async_copy(k_in.at[:, cols(h, DIM)], kv.at[2, y, co, 0, cols(h, PART), :], local.at[LK]),
        pltpu.make_async_copy(v_in.at[:, cols(h, DIM)], kv.at[2, y, co, 1, cols(h, PART), :], local.at[LV]),
        pltpu.make_async_copy(q_in.at[:, cols(h, COLS)], qs.at[cols(h, PART), :], local.at[LQ]),
        pltpu.make_async_copy(
            go_in.at[:, pl.ds(tile_row, 16), cols(tile_head, DIM)], gcol.at[pl.ds(2 * c, 2)], local.at[LG]
        ),
    ]
    for copy in local_copies:
        copy.start()

    barrier = pltpu.get_barrier_semaphore()

    def greet(step, carry):
        pl.semaphore_signal(barrier, inc=1, device_id=(lax.rem(c + step, N_CTX), h), device_id_type=MESH)
        return carry

    lax.fori_loop(1, N_CTX, greet, 0)
    for step in range(1, N_HEAD):
        pl.semaphore_signal(barrier, inc=1, device_id=(c, lax.rem(h + step, N_HEAD)), device_id_type=MESH)
    pl.semaphore_wait(barrier, N_CTX - 1 + N_HEAD - 1)

    for step in range(1, N_HEAD):
        to = lax.rem(h + step, N_HEAD)
        push(k_in.at[:, cols(to, DIM)], kv.at[2, y, co, 0, cols(h, PART), :], XK, c, to)
        push(v_in.at[:, cols(to, DIM)], kv.at[2, y, co, 1, cols(h, PART), :], XV, c, to)
    for step in range(1, N_HEAD):
        to = lax.rem(h + step, N_HEAD)
        push(q_in.at[:, cols(to, COLS)], qs.at[cols(h, PART), :], XQ, c, to)

    def tile_of(number):
        return pl.multiple_of(16 * (number // GROUP), 16), lax.rem(number, GROUP)

    def collect_grad(step, carry):
        to = lax.rem(c + step, N_CTX)
        row, head = tile_of(to)
        push(go_in.at[:, pl.ds(row, 16), cols(head, DIM)], gcol.at[pl.ds(2 * c, 2)], G1, to, h)
        return carry

    lax.fori_loop(1, N_CTX, collect_grad, 0)

    own = kv.at[2, y, co]
    local_copies[0].wait()
    local_copies[1].wait()
    drain(kv.at[2, y, co, 0, pl.ds(0, 3 * PART), :], recv.at[XK])
    drain(kv.at[2, y, co, 1, pl.ds(0, 3 * PART), :], recv.at[XV])
    push(own, kv.at[1, y, co], Z1, ctx_at(z + 1, y), h)
    push(own, kv.at[0, y, co], Z2, ctx_at(z + 2, y), h)

    def along_y(plane):
        for step in range(1, NY):
            push(kv.at[plane, y, co], kv.at[plane, y, co], Y0 + plane, ctx_at(z, y + step), h)

    along_y(2)

    local_copies[3].wait()
    drain(gcol.at[pl.ds(0, 62)], recv.at[G1])

    def arrange_grad(number, carry):
        gperm[number] = gcol[slot_of[number]]
        return carry

    lax.fori_loop(0, 2 * N_CTX, arrange_grad, 0)

    def deliver_grad(step, carry):
        to = lax.rem(c + step, N_CTX)
        push(
            gperm.at[pl.ds(2 * to, 2)], gos.at[tile_head, :, pl.ds(tile_row, 16), :], G2, to, h
        )
        return carry

    lax.fori_loop(1, N_CTX, deliver_grad, 0)
    gos[tile_head, :, pl.ds(tile_row, 16), :] = gperm[pl.ds(2 * c, 2)]

    drain(kv.at[1, y, co], recv.at[Z1])
    along_y(1)
    drain(kv.at[0, y, co], recv.at[Z2])
    along_y(0)
    for plane in (2, 1, 0):
        drain(kv.at[plane, pl.ds(0, 3), co], recv.at[Y0 + plane])
        push(kv.at[plane, :, co], kv.at[plane, :, co], C0 + plane, sib, h)

    local_copies[2].wait()
    drain(qs.at[pl.ds(0, 3 * PART), :], recv.at[XQ])
    for head in range(GROUP):
        rows = qs[:, head * DIM : (head + 1) * DIM]
        q_rows[head * TOK : (head + 1) * TOK, :] = rows
        q_cols[:, head * TOK : (head + 1) * TOK] = rows.T

    q_pos = c * TOK + lax.broadcasted_iota(jnp.int32, (1, TOK), 1)
    first = jnp.zeros((1, TOK), jnp.int32)
    begin = jnp.int32(0)
    for doc in range(NDOCS):
        first = jnp.where(q_pos >= begin, jnp.maximum(first, begin), first)
        begin = begin + doc_lengths[doc]

    parts[0] = jnp.zeros(parts.shape[1:], BF16)
    parts[2] = jnp.zeros(parts.shape[1:], BF16)

    for plane in (2, 1, 0):
        drain(kv.at[plane, :, co], recv.at[C0 + plane])

    def split(flat):
        return flat // PLANE, lax.rem(flat // NCORE, NY), lax.rem(flat, NCORE)

    def scores(step, peak):
        plane, yy, core = split(idx + step)
        keys = kv[plane, yy, core, 0]
        key_pos = (c - (WINDOW - 1) + step) * TOK + lax.broadcasted_iota(jnp.int32, (TOK, TOK), 0)
        bias = jnp.where((key_pos <= q_pos) & (key_pos >= first), 0.0, MASKED)
        bias = jnp.concatenate([bias] * GROUP, axis=1)
        block = jnp.dot(keys, q_cols[...], preferred_element_type=F32) * (SCALE * LOG2E) + bias
        probs[step] = block
        return jnp.maximum(peak, jnp.max(block, axis=0, keepdims=True))

    peak = lax.fori_loop(0, WINDOW, scores, jnp.full((1, ROWS), MASKED, F32))

    def attend(step, carry):
        total, accum = carry
        plane, yy, core = split(idx + step)
        values = kv[plane, yy, core, 1]
        block = jnp.exp2(probs[step] - peak)
        probs[step] = block
        total = total + jnp.sum(block, axis=0, keepdims=True)
        accum = accum + jnp.dot(values.T, block.astype(BF16), preferred_element_type=F32)
        return total, accum

    total, accum = lax.fori_loop(
        0, WINDOW, attend, (jnp.zeros((1, ROWS), F32), jnp.zeros((DIM, ROWS), F32))
    )
    inverse = 1.0 / total
    rounded = (accum * inverse).astype(BF16)
    for head in range(GROUP):
        rows = rounded[:, head * TOK : (head + 1) * TOK].T
        out_rows[head, 0] = rows[:64]
        out_rows[head, 1] = rows[64:]

    def collect_out(step, carry):
        to = lax.rem(c + step, N_CTX)
        row, head = tile_of(to)
        push(out_rows.at[head, :, pl.ds(row, 16), :], acol.at[pl.ds(2 * c, 2)], A1, to, h)
        return carry

    lax.fori_loop(1, N_CTX, collect_out, 0)
    acol[pl.ds(2 * c, 2)] = out_rows[tile_head, :, pl.ds(tile_row, 16), :]

    drain(gperm.at[pl.ds(0, 62)], recv.at[G2])
    for head in range(GROUP):
        go_cols[:, head * TOK : (head + 1) * TOK] = gos[head].reshape(TOK, DIM).T
    delta = jnp.sum(go_cols[...].astype(F32) * rounded.astype(F32), axis=0, keepdims=True)

    def backward(flat, query_grad):
        plane, yy, core = split(flat)
        keys, values = kv[plane, yy, core, 0], kv[plane, yy, core, 1]
        weights = probs[flat - idx] * inverse
        pushed = jnp.dot(values, go_cols[...], preferred_element_type=F32)
        slopes = (weights * (pushed - delta)).astype(BF16)
        go_rows = gos[...].reshape(ROWS, DIM)
        key_part = jnp.dot(slopes, q_rows[...], preferred_element_type=F32) * SCALE
        value_part = jnp.dot(weights.astype(BF16), go_rows, preferred_element_type=F32)
        parts[plane, yy, core, 0] = key_part.astype(BF16)
        parts[plane, yy, core, 1] = value_part.astype(BF16)
        return query_grad + jnp.dot(keys.T, slopes, preferred_element_type=F32)

    def to_core(plane):
        push(parts.at[plane, :, 1 - co], from_core.at[plane], CP + plane, sib, h)

    def to_y(plane):
        drain(from_core.at[plane], recv.at[CP + plane])
        mine = parts[plane, :, co].astype(F32) + from_core[plane].astype(F32)
        y_sum[plane] = mine.astype(BF16)
        for step in range(1, NY):
            other = lax.rem(y + step, NY)
            push(y_sum.at[plane, other], from_y.at[plane, step - 1], YP + plane, ctx_at(z, y + step), h)

    def sum_y(plane):
        drain(from_y.at[plane], recv.at[YP + plane])
        total = y_sum[plane, y].astype(F32)
        for step in range(NY - 1):
            total = total + from_y[plane, step].astype(F32)
        return total

    def to_z(plane):
        z_sum[plane] = sum_y(plane).astype(BF16)
        push(z_sum.at[plane], from_z.at[plane], ZP + plane, ctx_at(z + 2 + plane, y), h)

    query_grad = jnp.zeros((DIM, ROWS), F32)
    query_grad = lax.fori_loop(idx, PLANE, backward, query_grad)
    to_core(0)

    drain(acol.at[pl.ds(0, 62)], recv.at[A1])

    def arrange_out(number, carry):
        aperm[number] = acol[owned[number]]
        return carry

    lax.fori_loop(0, 2 * N_CTX, arrange_out, 0)

    def deliver_out(step, carry):
        to = lax.rem(c + step, N_CTX)
        push(
            aperm.at[pl.ds(2 * to, 2)], ao.at[:, pl.ds(tile_row, 16), cols(tile_head, DIM)], A2, to, h
        )
        return carry

    lax.fori_loop(1, N_CTX, deliver_out, 0)
    own_out = pltpu.make_async_copy(
        aperm.at[pl.ds(2 * c, 2)], ao.at[:, pl.ds(tile_row, 16), cols(tile_head, DIM)], local.at[LA]
    )
    own_out.start()

    query_grad = lax.fori_loop(PLANE, 2 * PLANE, backward, query_grad)
    to_core(1)
    to_y(0)
    query_grad = lax.fori_loop(2 * PLANE, 2 * PLANE + idx + 1, backward, query_grad)
    to_core(2)
    to_y(1)

    query_grad = (query_grad * SCALE).astype(BF16)
    for head in range(GROUP):
        dq_rows[:, head * DIM : (head + 1) * DIM] = query_grad[:, head * TOK : (head + 1) * TOK].T
    for step in range(1, N_HEAD):
        to = lax.rem(h + step, N_HEAD)
        push(dq_rows.at[cols(to, PART), :], gq.at[:, cols(h, COLS)], DQ, c, to)
    own_dq = pltpu.make_async_copy(dq_rows.at[cols(h, PART), :], gq.at[:, cols(h, COLS)], local.at[LDQ])
    own_dq.start()

    to_y(2)
    to_z(0)
    to_z(1)
    home = sum_y(2)
    for plane in (1, 0):
        drain(from_z.at[plane], recv.at[ZP + plane])
        home = home + from_z[plane].astype(F32)
    grads[...] = home.astype(BF16)
    for step in range(1, N_HEAD):
        to = lax.rem(h + step, N_HEAD)
        push(grads.at[0, cols(to, PART), :], gk.at[:, cols(h, DIM)], DK, c, to)
        push(grads.at[1, cols(to, PART), :], gv.at[:, cols(h, DIM)], DV, c, to)
    own_dk = pltpu.make_async_copy(grads.at[0, cols(h, PART), :], gk.at[:, cols(h, DIM)], local.at[LDK])
    own_dv = pltpu.make_async_copy(grads.at[1, cols(h, PART), :], gv.at[:, cols(h, DIM)], local.at[LDV])
    own_dk.start()
    own_dv.start()

    three_cols = pl.ds(0, 3 * COLS)
    drain(gperm.at[pl.ds(0, 62)], recv.at[A2])
    drain(gq.at[:, three_cols], recv.at[DQ])
    drain(gk.at[:, pl.ds(0, 3 * DIM)], recv.at[DK])
    drain(gv.at[:, pl.ds(0, 3 * DIM)], recv.at[DV])
    for copy in (own_out, own_dq, own_dk, own_dv):
        copy.wait()
    drain(kv.at[0, 0, 0, 0, pl.ds(0, 3 * PART), :], send.at[XK])
    drain(kv.at[0, 0, 0, 0, pl.ds(0, 3 * PART), :], send.at[XV])
    for sem in (G1, G2, A1, A2):
        drain(gperm.at[pl.ds(0, 62)], send.at[sem])
    for sem in (XQ, DQ):
        drain(gq.at[:, three_cols], send.at[sem])
    for sem in (DK, DV):
        drain(gk.at[:, pl.ds(0, 3 * DIM)], send.at[sem])
    for sem in (Z1, Z2, ZP, ZP + 1):
        drain(z_sum.at[0], send.at[sem])
    for plane in range(PLANES):
        drain(from_y.at[0], send.at[Y0 + plane])
        drain(from_y.at[0], send.at[YP + plane])
        drain(from_core.at[0], send.at[C0 + plane])
        drain(from_core.at[0], send.at[CP + plane])


def shards(queries, keys, values, grad_out, owner_lists, doc_lengths):
    owned = owner_lists.reshape(2 * N_CTX)
    slots = lax.iota(jnp.int32, 2 * N_CTX)
    slot_of = jnp.sum(jnp.where(owned[None, :] == slots[:, None], slots[None, :], 0), axis=1)
    hbm = pl.BlockSpec(memory_space=pl.ANY)
    smem = pl.BlockSpec(memory_space=pltpu.SMEM)
    block = (2, TOK, DIM)
    ao, gq, gk, gv = pl.pallas_call(
        body,
        out_shape=(
            jax.ShapeDtypeStruct((2, TOK // 2, COLS), BF16),
            jax.ShapeDtypeStruct((PART, N_HEAD * COLS), BF16),
            jax.ShapeDtypeStruct((PART, N_HEAD * DIM), BF16),
            jax.ShapeDtypeStruct((PART, N_HEAD * DIM), BF16),
        ),
        in_specs=[hbm] * 4 + [smem] * 3,
        out_specs=(hbm,) * 4,
        scratch_shapes=[
            pltpu.VMEM((PLANES, NY, NCORE) + block, BF16),
            pltpu.VMEM((TOK, COLS), BF16),
            pltpu.VMEM((2 * N_CTX, 16, DIM), BF16),
            pltpu.VMEM((2 * N_CTX, 16, DIM), BF16),
            pltpu.VMEM((GROUP, 2, TOK // 2, DIM), BF16),
            pltpu.VMEM((2 * N_CTX, 16, DIM), BF16),
            pltpu.VMEM((2 * N_CTX, 16, DIM), BF16),
            pltpu.VMEM((GROUP, 2, TOK // 2, DIM), BF16),
            pltpu.VMEM((TOK, COLS), BF16),
            pltpu.VMEM((ROWS, DIM), BF16),
            pltpu.VMEM((DIM, ROWS), BF16),
            pltpu.VMEM((DIM, ROWS), BF16),
            pltpu.VMEM((WINDOW, TOK, ROWS), F32),
            pltpu.VMEM((PLANES, NY, NCORE) + block, BF16),
            pltpu.VMEM((PLANES, NY) + block, BF16),
            pltpu.VMEM((PLANES, NY) + block, BF16),
            pltpu.VMEM((PLANES, NY - 1) + block, BF16),
            pltpu.VMEM((2,) + block, BF16),
            pltpu.VMEM((2,) + block, BF16),
            pltpu.VMEM(block, BF16),
            pltpu.SemaphoreType.DMA((N_SEM,)),
            pltpu.SemaphoreType.DMA((N_SEM,)),
            pltpu.SemaphoreType.DMA((N_LOCAL,)),
        ],
        compiler_params=pltpu.CompilerParams(
            collective_id=0, has_side_effects=True, vmem_limit_bytes=48 * 1024 * 1024
        ),
        cost_estimate=pl.CostEstimate(flops=4_000_000_000, bytes_accessed=4_000_000, transcendentals=2_300_000),
        name="attention_core",
    )(queries, keys, values, grad_out.reshape(2, TOK // 2, COLS), slot_of, owned, doc_lengths)
    return ao.reshape(TOK, COLS), gq, gk, gv


def solution(mesh):
    placed = (
        P(("ctx", "head"), None),
        P(("ctx", "head"), None),
        P(("ctx", "head"), None),
        P("ctx", "head"),
        P(),
        P(),
    )
    return jax.shard_map(
        shards,
        mesh=mesh,
        in_specs=placed,
        out_specs=(
            P("ctx", "head"),
            P(("ctx", "head"), None),
            P(("ctx", "head"), None),
            P(("ctx", "head"), None),
        ),
        check_vma=False,
    )
```

profile of v0, /device:TPU:1, one launch (start us, length us, event | category | flops | bytes accessed | tf_op | source)
XLA Modules:
  0.0 73.1 jit_solution(5854712690651691906)
XLA Ops:
  0.6 0.0 copy-start.5
  0.6 0.0 copy-start.2
  0.7 0.7 copy-done.5
  1.3 0.1 copy.12
  1.4 0.1 eq.15.owned
  1.5 0.0 copy-start.4
  1.5 0.1 select_reduce_fusion.slot_of
  1.6 0.0 copy-done.2
  1.6 0.5 copy-done.4
  2.2 0.0 copy-start
  2.2 0.9 %copy-done = bf16[32,4096]{1,0:T(8,128)(2,1)S(1)} copy-done((bf16[32,4096]{1,0:T(8,128)(2,1)S(1)}, bf16[32,4096]{1,0:T(8,128)(2,1)}, u32[]{:S(2)}) %copy-start) | copy-done | bytes 262168
  3.1 0.0 copy-start.1
  3.1 0.9 %copy-done.1 = bf16[128,1024]{1,0:T(8,128)(2,1)S(1)} copy-done((bf16[128,1024]{1,0:T(8,128)(2,1)S(1)}, bf16[128,1024]{1,0:T(8,128)(2,1)}, u32[]{:S(2)}) %copy-start.1) | copy-done | bytes 262168
  4.1 0.0 copy-start.3
  4.1 0.8 %copy-done.3 = bf16[32,512]{1,0:T(8,128)(2,1)S(1)} copy-done((bf16[32,512]{1,0:T(8,128)(2,1)S(1)}, bf16[32,512]{1,0:T(8,128)(2,1)}, u32[]{:S(2)}) %copy-start.3) | copy-done | bytes 32792
  4.8 65.6 %attention_core.1 = (bf16[2,64,1024]{2,1,0:T(8,128)(2,1)S(1)}, bf16[32,4096]{1,0:T(8,128)(2,1)S(1)}, bf16[32,512]{1,0:T(8,128)(2,1)S(1)}, bf16[32,512]{1,0:T(8,128)(2,1)S(1)}) custom-call(bf16[32,4096]{1,0:T(8,128)(2,1)S(1)} %copy-done, bf16[32,512]{1,0:T(8,128)(2,1)S(1)} %copy-done.2, bf16[32,512]{1,0:T(8,128)(2,1)S(1)} %copy-done.3, ...), custom_call_target="tpu_custom_call" | custom-call | flops 4000000000 | bytes 4000000 | tf_op jit(solution)/shard_map/attention_core/pallas_call | solution.py:346
  70.4 0.7 copy.17
  71.1 0.7 copy.18
  71.8 0.6 copy.19
  72.4 0.6 copy.20
Async XLA Ops:
  0.6 0.7 copy-start.5
  0.6 1.0 %copy-start.2 = (bf16[32,512]{1,0:T(8,128)(2,1)S(1)}, bf16[32,512]{1,0:T(8,128)(2,1)}, u32[]{:S(2)}) copy-start(bf16[32,512]{1,0:T(8,128)(2,1)} %k_in.1) | copy-start | bytes 98308
  1.5 0.7 copy-start.4
  2.2 0.9 %copy-start = (bf16[32,4096]{1,0:T(8,128)(2,1)S(1)}, bf16[32,4096]{1,0:T(8,128)(2,1)}, u32[]{:S(2)}) copy-start(bf16[32,4096]{1,0:T(8,128)(2,1)} %q_in.1) | copy-start | bytes 786436
  3.1 0.9 %copy-start.1 = (bf16[128,1024]{1,0:T(8,128)(2,1)S(1)}, bf16[128,1024]{1,0:T(8,128)(2,1)}, u32[]{:S(2)}) copy-start(bf16[128,1024]{1,0:T(8,128)(2,1)} %param.9) | copy-start | bytes 786436
  4.1 0.8 %copy-start.3 = (bf16[32,512]{1,0:T(8,128)(2,1)S(1)}, bf16[32,512]{1,0:T(8,128)(2,1)}, u32[]{:S(2)}) copy-start(bf16[32,512]{1,0:T(8,128)(2,1)} %v_in.1) | copy-start | bytes 98308
where the time goes:
time: 73.8 us; the launch traced here: 73.1 us
  Pallas kernels  65.6 us (89%)
  local copies, waits for them, and re-layouts  6.68 us (9%)
    pallas_call x1, Pallas kernels, shards(): pl.pallas_call(body, out_shape=(jax.ShapeDtypeStruct((2, TOK // 2, COLS),...  65.6 us
    unnamed x17, local copies, waits for them, and re-layouts  6.58 us

commit v1 on v0

v1 whole, which is shorter than its diff:
```python
import functools
import math

import jax
import jax.numpy as jnp
from jax import lax
from jax.experimental import pallas as pl
from jax.experimental.pallas import tpu as pltpu
from jax.sharding import PartitionSpec as P

MESH = pl.DeviceIdType.MESH
BF16 = jnp.bfloat16
F32 = jnp.float32

N_CTX, N_HEAD = 32, 4
NZ, NY, NCORE = 4, 4, 2
PLANE = NY * NCORE
PLANES = 3
SLOTS = 9
PAIR = 256
TOK = 128
PART = 32
DIM = 128
GROUP = 8
ROWS = TOK * GROUP
COLS = GROUP * DIM
NDOCS = 16
MASKED = -1e30
SCALE = 1.0 / math.sqrt(DIM)
LOG2E = 1.0 / math.log(2.0)

X0, X1, X2, Y1, YV, C1, CV, XQ, G1, G2, A1, A2, DQ, CP, YP1, YPV, XP = *range(14), 16, 17, 18
N_SEM = 21
LK, LV, LRK, LRV, LQ, LG, LA, LDQ, LDK, LDV = range(10)
N_LOCAL = 10


def body(
    q_in, k_in, v_in, go_in, owned, doc_lengths,
    ao, gq, gk, gv,
    raw, kv, qs, gcol, gperm, gos, acol, aperm, out_rows, dq_rows,
    q_rows, q_cols, go_cols, probs, parts, from_core, y_sum, from_y, x_sum, from_x, grads,
    slot_vec, slot_of, send, recv, local,
):
    c = lax.axis_index("ctx")
    h = lax.axis_index("head")
    z = c // PLANE
    idx = lax.rem(c, PLANE)
    y = idx // NCORE
    co = lax.rem(idx, NCORE)
    sib = c + 1 - 2 * co
    tile_row = pl.multiple_of(16 * (c // GROUP), 16)
    tile_head = lax.rem(c, GROUP)

    def ctx_at(zz, yy):
        return lax.rem(zz, NZ) * PLANE + lax.rem(yy, NY) * NCORE + co

    def push(src, dst, sem, ctx, head):
        copy = pltpu.make_async_remote_copy(
            src_ref=src, dst_ref=dst, send_sem=send.at[sem], recv_sem=recv.at[sem],
            device_id=(ctx, head), device_id_type=MESH,
        )
        copy.start()

    def drain(ref, sem):
        pltpu.make_async_copy(ref, ref, sem).wait()

    def cols(number, width):
        return pl.ds(pl.multiple_of(number * width, width), width)

    own_slot = NY + y

    local_copies = [
        pltpu.make_async_copy(k_in.at[:, cols(h, DIM)], kv.at[own_slot, co, 0, cols(h, PART), :], local.at[LK]),
        pltpu.make_async_copy(v_in.at[:, cols(h, DIM)], kv.at[own_slot, co, 1, cols(h, PART), :], local.at[LV]),
        pltpu.make_async_copy(k_in, raw.at[0], local.at[LRK]),
        pltpu.make_async_copy(v_in, raw.at[1], local.at[LRV]),
        pltpu.make_async_copy(q_in.at[:, cols(h, COLS)], qs.at[cols(h, PART), :], local.at[LQ]),
        pltpu.make_async_copy(
            go_in.at[:, pl.ds(tile_row, 16), cols(tile_head, DIM)], gcol.at[pl.ds(2 * c, 2)], local.at[LG]
        ),
    ]
    for copy in local_copies:
        copy.start()

    barrier = pltpu.get_barrier_semaphore()

    def greet(step, carry):
        pl.semaphore_signal(barrier, inc=1, device_id=(lax.rem(c + step, N_CTX), h), device_id_type=MESH)
        return carry

    lax.fori_loop(1, N_CTX, greet, 0)
    for step in range(1, N_HEAD):
        pl.semaphore_signal(barrier, inc=1, device_id=(c, lax.rem(h + step, N_HEAD)), device_id_type=MESH)
        for ahead in (1, 2, 3):
            pl.semaphore_signal(
                barrier, inc=1, device_id=(ctx_at(z + ahead, y), lax.rem(h + step, N_HEAD)), device_id_type=MESH
            )

    lanes = lax.broadcasted_iota(jnp.int32, (8, DIM), 1)
    found = jnp.zeros((8, DIM), jnp.int32)
    for number in range(2 * N_CTX):
        found = jnp.where(lanes == owned[number // 2, number % 2], number, found)
    slot_vec[...] = found
    slot_copy = pltpu.make_async_copy(slot_vec, slot_of, local.at[LA])
    slot_copy.start()

    for copy in local_copies[:4]:
        copy.wait()
    slot_copy.wait()
    pl.semaphore_wait(barrier, N_CTX - 1 + 4 * (N_HEAD - 1))

    def by_head(slot, sem, ctx, first_step):
        for step in range(first_step, N_HEAD):
            to = lax.rem(h + step, N_HEAD)
            push(raw.at[:, :, cols(to, DIM)], kv.at[slot, co, :, cols(h, PART), :], sem, ctx, to)

    by_head(own_slot, X0, c, 1)
    by_head(y, X1, ctx_at(z + 1, y), 0)
    by_head(2 * NY, X2, ctx_at(z + 2, y), 0)
    for step in range(1, N_HEAD):
        to = lax.rem(h + step, N_HEAD)
        push(q_in.at[:, cols(to, COLS)], qs.at[cols(h, PART), :], XQ, c, to)

    drain(kv.at[0, 0, :, pl.ds(0, 3 * PART), :], recv.at[X0])
    for step in range(1, NY):
        yy = lax.rem(y + step, NY)

        @pl.when(yy > y)
        def _():
            push(kv.at[own_slot, co], kv.at[own_slot, co], YV, ctx_at(z, yy), h)

    drain(kv.at[0, 0], recv.at[X1])
    for step in range(1, NY):
        push(kv.at[y, co], kv.at[y, co], Y1, ctx_at(z, y + step), h)
    drain(kv.at[0, 0], recv.at[X2])
    for step in range(1, NY):
        yy = lax.rem(y + step, NY)

        @pl.when(yy < y)
        def _():
            push(kv.at[2 * NY, co], kv.at[own_slot, co], YV, ctx_at(z, yy), h)

    def tile_of(number):
        return pl.multiple_of(16 * (number // GROUP), 16), lax.rem(number, GROUP)

    def collect_grad(step, carry):
        to = lax.rem(c + step, N_CTX)
        row, head = tile_of(to)
        push(go_in.at[:, pl.ds(row, 16), cols(head, DIM)], gcol.at[pl.ds(2 * c, 2)], G1, to, h)
        return carry

    lax.fori_loop(1, N_CTX, collect_grad, 0)

    local_copies[4].wait()
    drain(qs.at[pl.ds(0, 3 * PART), :], recv.at[XQ])
    for head in range(GROUP):
        rows = qs[:, head * DIM : (head + 1) * DIM]
        q_rows[head * TOK : (head + 1) * TOK, :] = rows
        q_cols[:, head * TOK : (head + 1) * TOK] = rows.T

    q_pos = c * TOK + lax.broadcasted_iota(jnp.int32, (1, TOK), 1)
    first = jnp.zeros((1, TOK), jnp.int32)
    begin = jnp.int32(0)
    for doc in range(NDOCS):
        first = jnp.where(q_pos >= begin, jnp.maximum(first, begin), first)
        begin = begin + doc_lengths[doc]

    drain(kv.at[pl.ds(0, 3), 0], recv.at[Y1])
    push(kv.at[pl.ds(0, NY), co], kv.at[pl.ds(0, NY), co], C1, sib, h)
    drain(kv.at[pl.ds(0, 3), 0], recv.at[YV])
    push(kv.at[pl.ds(NY, NY + 1), co], kv.at[pl.ds(NY, NY + 1), co], CV, sib, h)

    local_copies[5].wait()
    drain(gcol.at[pl.ds(0, 62)], recv.at[G1])

    def arrange_grad(number, carry):
        gperm[number] = gcol[slot_of[0, number]]
        return carry

    lax.fori_loop(0, 2 * N_CTX, arrange_grad, 0, unroll=8)

    def deliver_grad(step, carry):
        to = lax.rem(c + step, N_CTX)
        push(
            gperm.at[pl.ds(2 * to, 2)], gos.at[tile_head, :, pl.ds(tile_row, 16), :], G2, to, h
        )
        return carry

    lax.fori_loop(1, N_CTX, deliver_grad, 0)
    gos[tile_head, :, pl.ds(tile_row, 16), :] = gperm[pl.ds(2 * c, 2)]

    def position(slot):
        if slot < NY:
            return ((z - 1) * NY + slot) * PAIR
        if slot < 2 * NY:
            return (jnp.where(slot - NY <= y, z, z - 2) * NY + slot - NY) * PAIR
        return ((z - 2) * NY + y) * PAIR

    def scores(slot, peak):
        keys = kv[slot, :, 0].reshape(PAIR, DIM)
        key_pos = position(slot) + lax.broadcasted_iota(jnp.int32, (PAIR, TOK), 0)
        bias = jnp.where((key_pos <= q_pos) & (key_pos >= first), 0.0, MASKED)
        bias = jnp.concatenate([bias] * GROUP, axis=1)
        block = jnp.dot(keys, q_cols[...], preferred_element_type=F32) * (SCALE * LOG2E) + bias
        probs[slot] = block
        return jnp.maximum(peak, jnp.max(block.reshape(PAIR // 8, 8, ROWS), axis=0))

    peak = jnp.full((8, ROWS), MASKED, F32)
    drain(kv.at[pl.ds(0, NY), 0], recv.at[C1])
    for slot in range(NY):
        peak = scores(slot, peak)
    drain(kv.at[pl.ds(0, NY + 1), 0], recv.at[CV])
    for slot in range(NY, SLOTS):
        peak = scores(slot, peak)
    peak = jnp.max(peak, axis=0, keepdims=True)

    total = jnp.zeros((8, ROWS), F32)
    accum = jnp.zeros((DIM, ROWS), F32)
    for slot in range(SLOTS):
        values = kv[slot, :, 1].reshape(PAIR, DIM)
        block = jnp.exp2(probs[slot] - peak)
        probs[slot] = block
        total = total + jnp.sum(block.reshape(PAIR // 8, 8, ROWS), axis=0)
        accum = accum + jnp.dot(values.T, block.astype(BF16), preferred_element_type=F32)
    inverse = 1.0 / jnp.sum(total, axis=0, keepdims=True)
    rounded = (accum * inverse).astype(BF16)
    for head in range(GROUP):
        rows = rounded[:, head * TOK : (head + 1) * TOK].T
        out_rows[head, 0] = rows[:64]
        out_rows[head, 1] = rows[64:]

    def collect_out(step, carry):
        to = lax.rem(c + step, N_CTX)
        row, head = tile_of(to)
        push(out_rows.at[head, :, pl.ds(row, 16), :], acol.at[pl.ds(2 * c, 2)], A1, to, h)
        return carry

    lax.fori_loop(1, N_CTX, collect_out, 0)
    acol[pl.ds(2 * c, 2)] = out_rows[tile_head, :, pl.ds(tile_row, 16), :]

    drain(gperm.at[pl.ds(0, 62)], recv.at[G2])
    for head in range(GROUP):
        go_cols[:, head * TOK : (head + 1) * TOK] = gos[head].reshape(TOK, DIM).T
    delta = jnp.sum(go_cols[...].astype(F32) * rounded.astype(F32), axis=0, keepdims=True)

    def backward(slot, query_grad):
        keys, values = kv[slot, :, 0].reshape(PAIR, DIM), kv[slot, :, 1].reshape(PAIR, DIM)
        weights = probs[slot] * inverse
        pushed = jnp.dot(values, go_cols[...], preferred_element_type=F32)
        slopes = (weights * (pushed - delta)).astype(BF16)
        go_rows = gos[...].reshape(ROWS, DIM)
        key_part = jnp.dot(slopes, q_rows[...], preferred_element_type=F32) * SCALE
        value_part = jnp.dot(weights.astype(BF16), go_rows, preferred_element_type=F32)
        parts[slot, :, 0] = key_part.astype(BF16).reshape(NCORE, TOK, DIM)
        parts[slot, :, 1] = value_part.astype(BF16).reshape(NCORE, TOK, DIM)
        return query_grad + jnp.dot(keys.T, slopes, preferred_element_type=F32)

    def backward_group(slots, sem, query_grad):
        for slot in slots:
            query_grad = backward(slot, query_grad)
        for slot in slots:
            push(parts.at[slot, 1 - co], from_core.at[slot], sem, sib, h)
        return query_grad

    def both_cores(slot):
        return parts[slot, co].astype(F32) + from_core[slot].astype(F32)

    def to_y(slots, core_sem, number, sem):
        drain(from_core.at[pl.ds(0, 3)], recv.at[core_sem])
        for step, slot in enumerate(slots):
            y_sum[number, step] = both_cores(slot).astype(BF16)
            push(y_sum.at[number, step], from_y.at[number, step], sem, ctx_at(z, y + step + 1), h)

    beside = [lax.rem(y + step, NY) for step in range(1, NY)]
    virtual = [NY + yy for yy in beside]

    query_grad = jnp.zeros((DIM, ROWS), F32)
    query_grad = backward_group(beside, CP, query_grad)

    drain(acol.at[pl.ds(0, 62)], recv.at[A1])

    def arrange_out(number, carry):
        aperm[2 * number] = acol[owned[number, 0]]
        aperm[2 * number + 1] = acol[owned[number, 1]]
        return carry

    lax.fori_loop(0, N_CTX, arrange_out, 0, unroll=4)

    def deliver_out(step, carry):
        to = lax.rem(c + step, N_CTX)
        push(
            aperm.at[pl.ds(2 * to, 2)], ao.at[:, pl.ds(tile_row, 16), cols(tile_head, DIM)], A2, to, h
        )
        return carry

    lax.fori_loop(1, N_CTX, deliver_out, 0)
    own_out = pltpu.make_async_copy(
        aperm.at[pl.ds(2 * c, 2)], ao.at[:, pl.ds(tile_row, 16), cols(tile_head, DIM)], local.at[LA]
    )
    own_out.start()
    to_y(beside, CP, 0, YP1)

    query_grad = backward_group(virtual, CP + 1, query_grad)
    query_grad = backward_group([y, 2 * NY, own_slot], CP + 2, query_grad)
    to_y(virtual, CP + 1, 1, YPV)

    query_grad = (query_grad * SCALE).astype(BF16)
    for head in range(GROUP):
        dq_rows[:, head * DIM : (head + 1) * DIM] = query_grad[:, head * TOK : (head + 1) * TOK].T
    for step in range(1, N_HEAD):
        to = lax.rem(h + step, N_HEAD)
        push(dq_rows.at[cols(to, PART), :], gq.at[:, cols(h, COLS)], DQ, c, to)
    own_dq = pltpu.make_async_copy(dq_rows.at[cols(h, PART), :], gq.at[:, cols(h, COLS)], local.at[LDQ])
    own_dq.start()

    def home(plane, ctx, first_step):
        for step in range(first_step, N_HEAD):
            to = lax.rem(h + step, N_HEAD)
            push(x_sum.at[plane, :, cols(to, PART), :], from_x.at[plane, h], XP + plane, ctx, to)

    drain(from_core.at[pl.ds(0, 3)], recv.at[CP + 2])
    drain(from_y.at[0], recv.at[YP1])
    before = both_cores(y)
    for step in range(NY - 1):
        before = before + from_y[0, step].astype(F32)
    x_sum[1] = before.astype(BF16)
    home(1, ctx_at(z + 3, y), 0)
    drain(from_y.at[1], recv.at[YPV])
    oldest = both_cores(2 * NY)
    here = both_cores(own_slot)
    for step in range(1, NY):
        sender = lax.rem(y + NY - step, NY)
        piece = from_y[1, step - 1].astype(F32)
        here = here + jnp.where(sender > y, piece, 0.0)
        oldest = oldest + jnp.where(sender > y, 0.0, piece)
    x_sum[0] = oldest.astype(BF16)
    home(0, ctx_at(z + 2, y), 0)
    x_sum[2] = here.astype(BF16)
    home(2, c, 1)
    from_x[2, h] = x_sum[2, :, cols(h, PART), :]

    drain(from_x.at[1], recv.at[XP + 1])
    drain(from_x.at[0], recv.at[XP])
    drain(from_x.at[2, pl.ds(0, 3)], recv.at[XP + 2])
    for head in range(N_HEAD):
        piece = from_x[0, head].astype(F32) + from_x[1, head].astype(F32) + from_x[2, head].astype(F32)
        grads[:, :, head * DIM : (head + 1) * DIM] = piece.astype(BF16)
    own_dk = pltpu.make_async_copy(grads.at[0], gk, local.at[LDK])
    own_dv = pltpu.make_async_copy(grads.at[1], gv, local.at[LDV])
    own_dk.start()
    own_dv.start()

    three_cols = pl.ds(0, 3 * COLS)
    drain(gperm.at[pl.ds(0, 62)], recv.at[A2])
    drain(gq.at[:, three_cols], recv.at[DQ])
    for copy in (own_out, own_dq, own_dk, own_dv):
        copy.wait()
    for sem in (G1, G2, A1, A2):
        drain(gperm.at[pl.ds(0, 62)], send.at[sem])
    for sem in (XQ, DQ):
        drain(gq.at[:, three_cols], send.at[sem])
    for sem in (X0, XP + 2):
        drain(from_x.at[2, pl.ds(0, 3)], send.at[sem])
    for sem in (X1, X2, XP, XP + 1):
        drain(from_x.at[0], send.at[sem])
    for sem in (Y1, YV, YP1, YPV, CP, CP + 1, CP + 2):
        drain(from_y.at[0], send.at[sem])
    drain(kv.at[pl.ds(0, NY), 0], send.at[C1])
    drain(kv.at[pl.ds(0, NY + 1), 0], send.at[CV])


def shards(queries, keys, values, grad_out, owner_lists, doc_lengths):
    hbm = pl.BlockSpec(memory_space=pltpu.HBM)
    smem = pl.BlockSpec(memory_space=pltpu.SMEM)
    block = (2, TOK, DIM)
    piece = (2, PART, DIM)
    ao, gq, gk, gv = pl.pallas_call(
        body,
        out_shape=(
            jax.ShapeDtypeStruct((2, TOK // 2, COLS), BF16),
            jax.ShapeDtypeStruct((PART, N_HEAD * COLS), BF16),
            jax.ShapeDtypeStruct((PART, N_HEAD * DIM), BF16),
            jax.ShapeDtypeStruct((PART, N_HEAD * DIM), BF16),
        ),
        in_specs=[hbm] * 4 + [smem] * 2,
        out_specs=(hbm,) * 4,
        scratch_shapes=[
            pltpu.VMEM((2, PART, N_HEAD * DIM), BF16),
            pltpu.VMEM((SLOTS, NCORE) + block, BF16),
            pltpu.VMEM((TOK, COLS), BF16),
            pltpu.VMEM((2 * N_CTX, 16, DIM), BF16),
            pltpu.VMEM((2 * N_CTX, 16, DIM), BF16),
            pltpu.VMEM((GROUP, 2, TOK // 2, DIM), BF16),
            pltpu.VMEM((2 * N_CTX, 16, DIM), BF16),
            pltpu.VMEM((2 * N_CTX, 16, DIM), BF16),
            pltpu.VMEM((GROUP, 2, TOK // 2, DIM), BF16),
            pltpu.VMEM((TOK, COLS), BF16),
            pltpu.VMEM((ROWS, DIM), BF16),
            pltpu.VMEM((DIM, ROWS), BF16),
            pltpu.VMEM((DIM, ROWS), BF16),
            pltpu.VMEM((SLOTS, PAIR, ROWS), F32),
            pltpu.VMEM((SLOTS, NCORE) + block, BF16),
            pltpu.VMEM((SLOTS,) + block, BF16),
            pltpu.VMEM((2, NY - 1) + block, BF16),
            pltpu.VMEM((2, NY - 1) + block, BF16),
            pltpu.VMEM((PLANES,) + block, BF16),
            pltpu.VMEM((PLANES, N_HEAD) + piece, BF16),
            pltpu.VMEM((2, PART, N_HEAD * DIM), BF16),
            pltpu.VMEM((8, DIM), jnp.int32),
            pltpu.SMEM((8, DIM), jnp.int32),
            pltpu.SemaphoreType.DMA((N_SEM,)),
            pltpu.SemaphoreType.DMA((N_SEM,)),
            pltpu.SemaphoreType.DMA((N_LOCAL,)),
        ],
        compiler_params=pltpu.CompilerParams(
            collective_id=0, has_side_effects=True, vmem_limit_bytes=48 * 1024 * 1024
        ),
        cost_estimate=pl.CostEstimate(flops=4_000_000_000, bytes_accessed=4_000_000, transcendentals=2_300_000),
        name="attention_core",
    )(queries, keys, values, grad_out.reshape(2, TOK // 2, COLS), owner_lists, doc_lengths)
    return ao.reshape(TOK, COLS), gq, gk, gv


def solution(mesh):
    placed = (
        P(("ctx", "head"), None),
        P(("ctx", "head"), None),
        P(("ctx", "head"), None),
        P("ctx", "head"),
        P(),
        P(),
    )
    return jax.shard_map(
        shards,
        mesh=mesh,
        in_specs=placed,
        out_specs=(
            P("ctx", "head"),
            P(("ctx", "head"), None),
            P(("ctx", "head"), None),
            P(("ctx", "head"), None),
        ),
        check_vma=False,
    )
```

time: 73.8 us -> 61.1 us (0.83)
  Pallas kernels: 65.6 us -> 52.3 us
    pallas_call x1, Pallas kernels: 65.6 us -> 52.3 us  [shards(): pl.pallas_call(body, out_shape=(jax.ShapeDtypeStruct((2, TOK // 2, COLS),...]
    unnamed x17, local copies, waits for them, and re-layouts: 6.58 us -> 7.38 us
where the time goes in v1:
time: 61.1 us; the launch traced here: 60.4 us
  Pallas kernels  52.3 us (86%)
  local copies, waits for them, and re-layouts  7.38 us (12%)
  between operations  0.65 us (1%)
    pallas_call x1, Pallas kernels, shards(): pl.pallas_call(body, out_shape=(jax.ShapeDtypeStruct((2, TOK // 2, COLS),...  52.3 us
    unnamed x17, local copies, waits for them, and re-layouts  7.38 us

profile of v1, /device:TPU:1, one launch (start us, length us, event | category | flops | bytes accessed | tf_op | source)
XLA Modules:
  0.0 60.4 jit_solution(3389707712306762061)
XLA Ops:
  0.6 0.0 copy-start.5
  0.6 0.7 %copy-done.5 = s32[32,2]{0,1:T(2,128)S(1)} copy-done((s32[32,2]{0,1:T(2,128)S(1)}, s32[32,2]{0,1:T(2,128)}, u32[]{:S(2)}) %copy-start.5) | copy-done | bytes 280
  1.3 0.0 copy-start.4
  1.3 0.1 copy.10.owned
  1.4 0.6 copy-done.4
  2.0 0.0 copy-start
  2.0 0.9 %copy-done = bf16[32,4096]{1,0:T(8,128)(2,1)S(1)} copy-done((bf16[32,4096]{1,0:T(8,128)(2,1)S(1)}, bf16[32,4096]{1,0:T(8,128)(2,1)}, u32[]{:S(2)}) %copy-start) | copy-done | bytes 262168
  2.9 0.0 copy-start.1
  2.9 0.9 %copy-done.1 = bf16[128,1024]{1,0:T(8,128)(2,1)S(1)} copy-done((bf16[128,1024]{1,0:T(8,128)(2,1)S(1)}, bf16[128,1024]{1,0:T(8,128)(2,1)}, u32[]{:S(2)}) %copy-start.1) | copy-done | bytes 262168
  3.9 0.0 copy-start.2
  3.9 0.8 %copy-done.2 = bf16[32,512]{1,0:T(8,128)(2,1)S(1)} copy-done((bf16[32,512]{1,0:T(8,128)(2,1)S(1)}, bf16[32,512]{1,0:T(8,128)(2,1)}, u32[]{:S(2)}) %copy-start.2) | copy-done | bytes 32792
  4.6 0.0 copy-start.3
  4.6 0.8 %copy-done.3 = bf16[32,512]{1,0:T(8,128)(2,1)S(1)} copy-done((bf16[32,512]{1,0:T(8,128)(2,1)S(1)}, bf16[32,512]{1,0:T(8,128)(2,1)}, u32[]{:S(2)}) %copy-start.3) | copy-done | bytes 32792
  5.4 52.3 %attention_core.1 = (bf16[2,64,1024]{2,1,0:T(8,128)(2,1)S(1)}, bf16[32,4096]{1,0:T(8,128)(2,1)S(1)}, bf16[32,512]{1,0:T(8,128)(2,1)S(1)}, bf16[32,512]{1,0:T(8,128)(2,1)S(1)}) custom-call(bf16[32,4096]{1,0:T(8,128)(2,1)S(1)} %copy-done, bf16[32,512]{1,0:T(8,128)(2,1)S(1)} %copy-done.2, bf16[32,512]{1,0:T(8,128)(2,1)S(1)} %copy-done.3, ...), custom_call_target="tpu_custom_call" | custom-call | flops 4000000000 | bytes 4000000 | tf_op jit(solution)/shard_map/attention_core/pallas_call | solution.py:378
  57.7 0.7 %copy.15 = bf16[128,1024]{1,0:T(8,128)(2,1)} copy(bf16[128,1024]{1,0:T(8,128)(2,1)S(1)} %bitcast.2) | data formatting | bytes 524288
  58.4 0.7 %copy.16 = bf16[32,4096]{1,0:T(8,128)(2,1)} copy(bf16[32,4096]{1,0:T(8,128)(2,1)S(1)} %get-tuple-element.17) | data formatting | bytes 524288
  59.1 0.6 %copy.17 = bf16[32,512]{1,0:T(8,128)(2,1)} copy(bf16[32,512]{1,0:T(8,128)(2,1)S(1)} %get-tuple-element.18) | data formatting | bytes 65536
  59.8 0.6 %copy.18 = bf16[32,512]{1,0:T(8,128)(2,1)} copy(bf16[32,512]{1,0:T(8,128)(2,1)S(1)} %get-tuple-element.19) | data formatting | bytes 65536
Async XLA Ops:
  0.6 0.7 %copy-start.5 = (s32[32,2]{0,1:T(2,128)S(1)}, s32[32,2]{0,1:T(2,128)}, u32[]{:S(2)}) copy-start(s32[32,2]{0,1:T(2,128)} %param.10) | copy-start | bytes 772
  1.3 0.7 %copy-start.4 = (s32[16]{0:T(128)S(1)}, s32[16]{0:T(128)}, u32[]{:S(2)}) copy-start(s32[16]{0:T(128)} %doc_lengths.1) | copy-start | bytes 196
  2.0 0.9 %copy-start = (bf16[32,4096]{1,0:T(8,128)(2,1)S(1)}, bf16[32,4096]{1,0:T(8,128)(2,1)}, u32[]{:S(2)}) copy-start(bf16[32,4096]{1,0:T(8,128)(2,1)} %q_in.1) | copy-start | bytes 786436
  2.9 0.9 %copy-start.1 = (bf16[128,1024]{1,0:T(8,128)(2,1)S(1)}, bf16[128,1024]{1,0:T(8,128)(2,1)}, u32[]{:S(2)}) copy-start(bf16[128,1024]{1,0:T(8,128)(2,1)} %param.9) | copy-start | bytes 786436
  3.9 0.8 %copy-start.2 = (bf16[32,512]{1,0:T(8,128)(2,1)S(1)}, bf16[32,512]{1,0:T(8,128)(2,1)}, u32[]{:S(2)}) copy-start(bf16[32,512]{1,0:T(8,128)(2,1)} %k_in.1) | copy-start | bytes 98308
  4.6 0.8 %copy-start.3 = (bf16[32,512]{1,0:T(8,128)(2,1)S(1)}, bf16[32,512]{1,0:T(8,128)(2,1)}, u32[]{:S(2)}) copy-start(bf16[32,512]{1,0:T(8,128)(2,1)} %v_in.1) | copy-start | bytes 98308

commit v2 on v1

--- a/solution.py
+++ b/solution.py
@@ -100,7 +100,7 @@
     lanes = lax.broadcasted_iota(jnp.int32, (8, DIM), 1)
     found = jnp.zeros((8, DIM), jnp.int32)
     for number in range(2 * N_CTX):
-        found = jnp.where(lanes == owned[number // 2, number % 2], number, found)
+        found = jnp.where(lanes == owned[number % 2, number // 2], number, found)
     slot_vec[...] = found
     slot_copy = pltpu.make_async_copy(slot_vec, slot_of, local.at[LA])
     slot_copy.start()
@@ -118,6 +118,17 @@
     by_head(own_slot, X0, c, 1)
     by_head(y, X1, ctx_at(z + 1, y), 0)
     by_head(2 * NY, X2, ctx_at(z + 2, y), 0)
+    def tile_of(number):
+        return pl.multiple_of(16 * (number // GROUP), 16), lax.rem(number, GROUP)
+
+    def collect_grad(step, carry):
+        to = lax.rem(c + step, N_CTX)
+        row, head = tile_of(to)
+        push(go_in.at[:, pl.ds(row, 16), cols(head, DIM)], gcol.at[pl.ds(2 * c, 2)], G1, to, h)
+        return carry
+
+    lax.fori_loop(1, N_CTX, collect_grad, 0)
+
     for step in range(1, N_HEAD):
         to = lax.rem(h + step, N_HEAD)
         push(q_in.at[:, cols(to, COLS)], qs.at[cols(h, PART), :], XQ, c, to)
@@ -141,16 +152,24 @@
         def _():
             push(kv.at[2 * NY, co], kv.at[own_slot, co], YV, ctx_at(z, yy), h)
 
-    def tile_of(number):
-        return pl.multiple_of(16 * (number // GROUP), 16), lax.rem(number, GROUP)
-
-    def collect_grad(step, carry):
+    local_copies[5].wait()
+    drain(gcol.at[pl.ds(0, 62)], recv.at[G1])
+
+    def arrange_grad(number, carry):
+        gperm[number] = gcol[slot_of[0, number]]
+        return carry
+
+    lax.fori_loop(0, 2 * N_CTX, arrange_grad, 0, unroll=8)
+
+    def deliver_grad(step, carry):
         to = lax.rem(c + step, N_CTX)
-        row, head = tile_of(to)
-        push(go_in.at[:, pl.ds(row, 16), cols(head, DIM)], gcol.at[pl.ds(2 * c, 2)], G1, to, h)
-        return carry
-
-    lax.fori_loop(1, N_CTX, collect_grad, 0)
+        push(
+            gperm.at[pl.ds(2 * to, 2)], gos.at[tile_head, :, pl.ds(tile_row, 16), :], G2, to, h
+        )
+        return carry
+
+    lax.fori_loop(1, N_CTX, deliver_grad, 0)
+    gos[tile_head, :, pl.ds(tile_row, 16), :] = gperm[pl.ds(2 * c, 2)]
 
     local_copies[4].wait()
     drain(qs.at[pl.ds(0, 3 * PART), :], recv.at[XQ])
@@ -170,25 +189,6 @@
     push(kv.at[pl.ds(0, NY), co], kv.at[pl.ds(0, NY), co], C1, sib, h)
     drain(kv.at[pl.ds(0, 3), 0], recv.at[YV])
     push(kv.at[pl.ds(NY, NY + 1), co], kv.at[pl.ds(NY, NY + 1), co], CV, sib, h)
-
-    local_copies[5].wait()
-    drain(gcol.at[pl.ds(0, 62)], recv.at[G1])
-
-    def arrange_grad(number, carry):
-        gperm[number] = gcol[slot_of[0, number]]
-        return carry
-
-    lax.fori_loop(0, 2 * N_CTX, arrange_grad, 0, unroll=8)
-
-    def deliver_grad(step, carry):
-        to = lax.rem(c + step, N_CTX)
-        push(
-            gperm.at[pl.ds(2 * to, 2)], gos.at[tile_head, :, pl.ds(tile_row, 16), :], G2, to, h
-        )
-        return carry
-
-    lax.fori_loop(1, N_CTX, deliver_grad, 0)
-    gos[tile_head, :, pl.ds(tile_row, 16), :] = gperm[pl.ds(2 * c, 2)]
 
     def position(slot):
         if slot < NY:
@@ -278,30 +278,8 @@
     query_grad = jnp.zeros((DIM, ROWS), F32)
     query_grad = backward_group(beside, CP, query_grad)
 
-    drain(acol.at[pl.ds(0, 62)], recv.at[A1])
-
-    def arrange_out(number, carry):
-        aperm[2 * number] = acol[owned[number, 0]]
-        aperm[2 * number + 1] = acol[owned[number, 1]]
-        return carry
-
-    lax.fori_loop(0, N_CTX, arrange_out, 0, unroll=4)
-
-    def deliver_out(step, carry):
-        to = lax.rem(c + step, N_CTX)
-        push(
-            aperm.at[pl.ds(2 * to, 2)], ao.at[:, pl.ds(tile_row, 16), cols(tile_head, DIM)], A2, to, h
-        )
-        return carry
-
-    lax.fori_loop(1, N_CTX, deliver_out, 0)
-    own_out = pltpu.make_async_copy(
-        aperm.at[pl.ds(2 * c, 2)], ao.at[:, pl.ds(tile_row, 16), cols(tile_head, DIM)], local.at[LA]
-    )
-    own_out.start()
+    query_grad = backward_group(virtual, CP + 1, query_grad)
     to_y(beside, CP, 0, YP1)
-
-    query_grad = backward_group(virtual, CP + 1, query_grad)
     query_grad = backward_group([y, 2 * NY, own_slot], CP + 2, query_grad)
     to_y(virtual, CP + 1, 1, YPV)
 
@@ -314,6 +292,27 @@
     own_dq = pltpu.make_async_copy(dq_rows.at[cols(h, PART), :], gq.at[:, cols(h, COLS)], local.at[LDQ])
     own_dq.start()
 
+    drain(acol.at[pl.ds(0, 62)], recv.at[A1])
+
+    def arrange_out(number, carry):
+        aperm[2 * number] = acol[owned[0, number]]
+        aperm[2 * number + 1] = acol[owned[1, number]]
+        return carry
+
+    lax.fori_loop(0, N_CTX, arrange_out, 0, unroll=4)
+
+    def deliver_out(step, carry):
+        to = lax.rem(c + step, N_CTX)
+        push(
+            aperm.at[pl.ds(2 * to, 2)], ao.at[:, pl.ds(tile_row, 16), cols(tile_head, DIM)], A2, to, h
+        )
+        return carry
+
+    lax.fori_loop(1, N_CTX, deliver_out, 0)
+    own_out = pltpu.make_async_copy(
+        aperm.at[pl.ds(2 * c, 2)], ao.at[:, pl.ds(tile_row, 16), cols(tile_head, DIM)], local.at[LA]
+    )
+    own_out.start()
     def home(plane, ctx, first_step):
         for step in range(first_step, N_HEAD):
             to = lax.rem(h + step, N_HEAD)
@@ -368,6 +367,30 @@
         drain(from_y.at[0], send.at[sem])
     drain(kv.at[pl.ds(0, NY), 0], send.at[C1])
     drain(kv.at[pl.ds(0, NY + 1), 0], send.at[CV])
+
+
+def finish_body(ao, gq, gk, gv, ao_out, gq_out, gk_out, gv_out, sems):
+    copies = [
+        pltpu.make_async_copy(src, dst, sems.at[number])
+        for number, (src, dst) in enumerate(((ao, ao_out), (gq, gq_out), (gk, gk_out), (gv, gv_out)))
+    ]
+    for copy in copies:
+        copy.start()
+    for copy in copies:
+        copy.wait()
+
+
+def finish(*arrays):
+    anywhere = pl.BlockSpec(memory_space=pltpu.VMEM)
+    hbm = pl.BlockSpec(memory_space=pltpu.HBM)
+    return pl.pallas_call(
+        finish_body,
+        out_shape=tuple(jax.ShapeDtypeStruct(array.shape, array.dtype) for array in arrays),
+        in_specs=[anywhere] * 4,
+        out_specs=(hbm,) * 4,
+        scratch_shapes=[pltpu.SemaphoreType.DMA((4,))],
+        name="write_outputs",
+    )(*arrays)
 
 
 def shards(queries, keys, values, grad_out, owner_lists, doc_lengths):
@@ -414,12 +437,12 @@
             pltpu.SemaphoreType.DMA((N_LOCAL,)),
         ],
         compiler_params=pltpu.CompilerParams(
-            collective_id=0, has_side_effects=True, vmem_limit_bytes=48 * 1024 * 1024
+            collective_id=0, has_side_effects=True, vmem_limit_bytes=56 * 1024 * 1024
         ),
         cost_estimate=pl.CostEstimate(flops=4_000_000_000, bytes_accessed=4_000_000, transcendentals=2_300_000),
         name="attention_core",
-    )(queries, keys, values, grad_out.reshape(2, TOK // 2, COLS), owner_lists, doc_lengths)
-    return ao.reshape(TOK, COLS), gq, gk, gv
+    )(queries, keys, values, grad_out.reshape(2, TOK // 2, COLS), owner_lists.T, doc_lengths)
+    return finish(ao.reshape(TOK, COLS), gq, gk, gv)
 
 
 def solution(mesh):

time: 61.1 us -> 48.8 us (0.80)
  local copies, waits for them, and re-layouts: 7.38 us -> 0 us
  Pallas kernels: 52.3 us -> 48 us
    unnamed x17 -> x0, local copies, waits for them, and re-layouts: 7.38 us -> none
    pallas_call x1, Pallas kernels: 52.3 us -> 46.1 us  [shards(): pl.pallas_call(body, out_shape=(jax.ShapeDtypeStruct((2, TOK // 2, COLS),...]
    pallas_call x0 -> x1, Pallas kernels: none -> 1.87 us  [finish(): pl.pallas_call(finish_body, out_shape=tuple((jax.ShapeDtypeStruct(array.s...]
where the time goes in v2:
time: 48.8 us; the launch traced here: 48.6 us
  Pallas kernels  48 us (98%)
  between operations  0.64 us (1%)
    pallas_call x1, Pallas kernels, shards(): pl.pallas_call(body, out_shape=(jax.ShapeDtypeStruct((2, TOK // 2, COLS),...  46.1 us
    pallas_call x1, Pallas kernels, finish(): pl.pallas_call(finish_body, out_shape=tuple((jax.ShapeDtypeStruct(array.s...  1.87 us

profile of v2, /device:TPU:1, one launch (start us, length us, event | category | flops | bytes accessed | tf_op | source)
XLA Modules:
  0.0 48.6 jit_solution(2731001297374454955)
XLA Ops:
  0.6 46.1 %attention_core.1 = (bf16[2,64,1024]{2,1,0:T(8,128)(2,1)}, bf16[32,4096]{1,0:T(8,128)(2,1)}, bf16[32,512]{1,0:T(8,128)(2,1)}, bf16[32,512]{1,0:T(8,128)(2,1)}) custom-call(bf16[32,4096]{1,0:T(8,128)(2,1)} %q_in.1, bf16[32,512]{1,0:T(8,128)(2,1)} %k_in.1, bf16[32,512]{1,0:T(8,128)(2,1)} %v_in.1, bf16[2,64,1024]{2,1,0:T(8,128)(2,1)} %bitcast.4, ...), custom_call_target="tpu_custom_call" | custom-call | flops 4000000000 | bytes 4000000 | tf_op jit(solution)/shard_map/attention_core/pallas_call | solution.py:401
  46.7 1.9 %write_outputs.1 = (bf16[128,1024]{1,0:T(8,128)(2,1)}, bf16[32,4096]{1,0:T(8,128)(2,1)}, bf16[32,512]{1,0:T(8,128)(2,1)}, bf16[32,512]{1,0:T(8,128)(2,1)}) custom-call(bf16[128,1024]{1,0:T(8,128)(2,1)} %bitcast.3, bf16[32,4096]{1,0:T(8,128)(2,1)} %get-tuple-element.9.gq, bf16[32,512]{1,0:T(8,128)(2,1)} %get-tuple-element.10.gk, ...), custom_call_target="tpu_custom_call" | custom-call | tf_op jit(solution)/shard_map/write_outputs/pallas_call | solution.py:386

commit v3 on v2

v3 whole, which is shorter than its diff:
```python
import functools
import math

import jax
import jax.numpy as jnp
from jax import lax
from jax.experimental import pallas as pl
from jax.experimental.pallas import tpu as pltpu
from jax.sharding import PartitionSpec as P

MESH = pl.DeviceIdType.MESH
BF16 = jnp.bfloat16
F32 = jnp.float32

N_CTX, N_HEAD = 32, 4
NZ, NY, NCORE = 4, 4, 2
PLANE = NY * NCORE
PLANES = 3
SLOTS = 9
PAIR = 256
TOK = 128
PART = 32
DIM = 128
GROUP = 8
ROWS = TOK * GROUP
COLS = GROUP * DIM
NDOCS = 16
MASKED = -1e30
SCALE = 1.0 / math.sqrt(DIM)
LOG2E = 1.0 / math.log(2.0)

XQ, G1, G2, A1, A2, DQ = range(6)
X0, X1, X2, Y1, YV, C1, CV, YP, XPV, XP, CP = (6, 8, 10, 12, 14, 16, 18, 20, 22, 24, 30)
N_SEM = 36
LK, LV, LRK, LRV, LQ, LG, LA, LDQ, LDK, LDV = range(10)
N_LOCAL = 10


def body(
    q_in, k_in, v_in, go_in, owned, doc_lengths,
    ao, gq, gk, gv,
    raw, kv, qs, gcol, gperm, gos, acol, aperm, out_rows, dq_rows,
    q_rows, q_cols, go_cols, probs, rounded_probs, parts, from_core, y_sum, from_y, sums, from_x, grads,
    slot_vec, slot_of, send, recv, local,
):
    c = lax.axis_index("ctx")
    h = lax.axis_index("head")
    z = c // PLANE
    idx = lax.rem(c, PLANE)
    y = idx // NCORE
    co = lax.rem(idx, NCORE)
    sib = c + 1 - 2 * co
    tile_row = pl.multiple_of(16 * (c // GROUP), 16)
    tile_head = lax.rem(c, GROUP)

    def ctx_at(zz, yy):
        return lax.rem(zz, NZ) * PLANE + lax.rem(yy, NY) * NCORE + co

    def push(src, dst, sem, ctx, head):
        copy = pltpu.make_async_remote_copy(
            src_ref=src, dst_ref=dst, send_sem=send.at[sem], recv_sem=recv.at[sem],
            device_id=(ctx, head), device_id_type=MESH,
        )
        copy.start()

    def drain(ref, sem):
        pltpu.make_async_copy(ref, ref, sem).wait()

    def cols(number, width):
        return pl.ds(pl.multiple_of(number * width, width), width)

    own_slot = NY + y

    local_copies = [
        pltpu.make_async_copy(k_in.at[:, cols(h, DIM)], kv.at[0, own_slot, co, cols(h, PART), :], local.at[LK]),
        pltpu.make_async_copy(v_in.at[:, cols(h, DIM)], kv.at[1, own_slot, co, cols(h, PART), :], local.at[LV]),
        pltpu.make_async_copy(k_in, raw.at[0], local.at[LRK]),
        pltpu.make_async_copy(v_in, raw.at[1], local.at[LRV]),
        pltpu.make_async_copy(q_in.at[:, cols(h, COLS)], qs.at[cols(h, PART), :], local.at[LQ]),
        pltpu.make_async_copy(
            go_in.at[:, pl.ds(tile_row, 16), cols(tile_head, DIM)], gcol.at[pl.ds(2 * c, 2)], local.at[LG]
        ),
    ]
    for copy in local_copies:
        copy.start()

    barrier = pltpu.get_barrier_semaphore()

    def greet(step, carry):
        pl.semaphore_signal(barrier, inc=1, device_id=(lax.rem(c + step, N_CTX), h), device_id_type=MESH)
        return carry

    lax.fori_loop(1, N_CTX, greet, 0)
    def greet_heads(ctx):
        for step in range(1, N_HEAD):
            pl.semaphore_signal(barrier, inc=1, device_id=(ctx, lax.rem(h + step, N_HEAD)), device_id_type=MESH)

    for ahead in range(NZ):
        greet_heads(ctx_at(z + ahead, y))
    for step in range(1, NY):
        greet_heads(ctx_at(z, y + step))
        greet_heads(ctx_at(z + 2, y + step))

    lanes = lax.broadcasted_iota(jnp.int32, (8, DIM), 1)
    found = jnp.zeros((8, DIM), jnp.int32)
    for number in range(2 * N_CTX):
        found = jnp.where(lanes == owned[number % 2, number // 2], number, found)
    slot_vec[...] = found
    slot_copy = pltpu.make_async_copy(slot_vec, slot_of, local.at[LA])
    slot_copy.start()

    for copy in local_copies[:4]:
        copy.wait()
    slot_copy.wait()
    pl.semaphore_wait(barrier, N_CTX - 1 + (NZ + 2 * (NY - 1)) * (N_HEAD - 1))

    def tile_of(number):
        return pl.multiple_of(16 * (number // GROUP), 16), lax.rem(number, GROUP)

    def collect_grad(step, carry):
        to = lax.rem(c + step, N_CTX)
        row, head = tile_of(to)
        push(go_in.at[:, pl.ds(row, 16), cols(head, DIM)], gcol.at[pl.ds(2 * c, 2)], G1, to, h)
        return carry

    lax.fori_loop(1, N_CTX, collect_grad, 0)

    def by_head(which, slot, sem, ctx, first_step):
        for step in range(first_step, N_HEAD):
            to = lax.rem(h + step, N_HEAD)
            push(
                raw.at[which, :, cols(to, DIM)], kv.at[which, slot, co, cols(h, PART), :], sem + which, ctx, to
            )

    def first_hop(which):
        by_head(which, y, X1, ctx_at(z + 1, y), 0)
        by_head(which, 2 * NY, X2, ctx_at(z + 2, y), 0)
        by_head(which, own_slot, X0, c, 1)
        for step in range(1, NY):
            yy = lax.rem(y + step, NY)

            @pl.when(yy > y)
            def _():
                by_head(which, own_slot, YV, ctx_at(z, yy), 0)

    first_hop(0)
    for step in range(1, N_HEAD):
        to = lax.rem(h + step, N_HEAD)
        push(q_in.at[:, cols(to, COLS)], qs.at[cols(h, PART), :], XQ, c, to)
    first_hop(1)

    def along_y(which):
        drain(kv.at[0, 0, 0], recv.at[X1 + which])
        for step in range(1, NY):
            push(kv.at[which, y, co], kv.at[which, y, co], Y1 + which, ctx_at(z, y + step), h)
        drain(kv.at[0, 0, 0], recv.at[X2 + which])
        for step in range(1, NY):
            yy = lax.rem(y + step, NY)

            @pl.when(yy < y)
            def _():
                push(kv.at[which, 2 * NY, co], kv.at[which, own_slot, co], YV + which, ctx_at(z, yy), h)

    along_y(0)
    along_y(1)

    q_pos = c * TOK + lax.broadcasted_iota(jnp.int32, (1, TOK), 1)
    first = jnp.zeros((1, TOK), jnp.int32)
    begin = jnp.int32(0)
    for doc in range(NDOCS):
        first = jnp.where(q_pos >= begin, jnp.maximum(first, begin), first)
        begin = begin + doc_lengths[doc]

    local_copies[5].wait()
    drain(gcol.at[pl.ds(0, 62)], recv.at[G1])

    def arrange_grad(number, carry):
        gperm[number] = gcol[slot_of[0, number]]
        return carry

    lax.fori_loop(0, 2 * N_CTX, arrange_grad, 0, unroll=8)

    def deliver_grad(step, carry):
        to = lax.rem(c + step, N_CTX)
        push(
            gperm.at[pl.ds(2 * to, 2)], gos.at[tile_head, :, pl.ds(tile_row, 16), :], G2, to, h
        )
        return carry

    lax.fori_loop(1, N_CTX, deliver_grad, 0)
    gos[tile_head, :, pl.ds(tile_row, 16), :] = gperm[pl.ds(2 * c, 2)]

    local_copies[4].wait()
    drain(qs.at[pl.ds(0, 3 * PART), :], recv.at[XQ])
    for head in range(GROUP):
        rows = qs[:, head * DIM : (head + 1) * DIM]
        q_rows[head * TOK : (head + 1) * TOK, :] = rows
        q_cols[:, head * TOK : (head + 1) * TOK] = rows.T

    def to_other_core(which):
        drain(kv.at[0, pl.ds(0, 3), 0], recv.at[Y1 + which])
        push(kv.at[which, pl.ds(0, NY), co], kv.at[which, pl.ds(0, NY), co], C1 + which, sib, h)
        drain(kv.at[0, 0, 0, pl.ds(0, 3 * PART), :], recv.at[X0 + which])
        drain(kv.at[0, pl.ds(0, 3), 0], recv.at[YV + which])
        push(kv.at[which, pl.ds(NY, NY + 1), co], kv.at[which, pl.ds(NY, NY + 1), co], CV + which, sib, h)

    to_other_core(0)

    def position(slot):
        if slot < NY:
            return ((z - 1) * NY + slot) * PAIR
        if slot < 2 * NY:
            return (jnp.where(slot - NY <= y, z, z - 2) * NY + slot - NY) * PAIR
        return ((z - 2) * NY + y) * PAIR

    def scores(slot, peak):
        keys = kv[0, slot].reshape(PAIR, DIM)
        key_pos = position(slot) + lax.broadcasted_iota(jnp.int32, (PAIR, TOK), 0)
        bias = jnp.where((key_pos <= q_pos) & (key_pos >= first), 0.0, MASKED)
        bias = jnp.concatenate([bias] * GROUP, axis=1)
        block = jnp.dot(keys, q_cols[...], preferred_element_type=F32) * (SCALE * LOG2E) + bias
        probs[slot] = block
        return jnp.maximum(peak, jnp.max(block.reshape(PAIR // 8, 8, ROWS), axis=0))

    peak = jnp.full((8, ROWS), MASKED, F32)
    drain(kv.at[0, pl.ds(0, NY), 0], recv.at[C1])
    for slot in range(NY):
        peak = scores(slot, peak)
    drain(kv.at[0, pl.ds(0, NY + 1), 0], recv.at[CV])
    for slot in range(NY, SLOTS):
        peak = scores(slot, peak)
    peak = jnp.max(peak, axis=0, keepdims=True)
    to_other_core(1)

    total = jnp.zeros((8, ROWS), F32)
    for slot in range(SLOTS):
        block = jnp.exp2(probs[slot] - peak)
        probs[slot] = block
        rounded_probs[slot] = block.astype(BF16)
        total = total + jnp.sum(block.reshape(PAIR // 8, 8, ROWS), axis=0)
    drain(kv.at[0, pl.ds(0, NY), 0], recv.at[C1 + 1])
    drain(kv.at[0, pl.ds(0, NY + 1), 0], recv.at[CV + 1])
    accum = jnp.zeros((DIM, ROWS), F32)
    for slot in range(SLOTS):
        values = kv[1, slot].reshape(PAIR, DIM)
        accum = accum + jnp.dot(values.T, rounded_probs[slot], preferred_element_type=F32)
    inverse = 1.0 / jnp.sum(total, axis=0, keepdims=True)
    rounded = (accum * inverse).astype(BF16)
    for head in range(GROUP):
        rows = rounded[:, head * TOK : (head + 1) * TOK].T
        out_rows[head, 0] = rows[:64]
        out_rows[head, 1] = rows[64:]

    def collect_out(step, carry):
        to = lax.rem(c + step, N_CTX)
        row, head = tile_of(to)
        push(out_rows.at[head, :, pl.ds(row, 16), :], acol.at[pl.ds(2 * c, 2)], A1, to, h)
        return carry

    lax.fori_loop(1, N_CTX, collect_out, 0)
    acol[pl.ds(2 * c, 2)] = out_rows[tile_head, :, pl.ds(tile_row, 16), :]

    drain(gperm.at[pl.ds(0, 62)], recv.at[G2])
    for head in range(GROUP):
        go_cols[:, head * TOK : (head + 1) * TOK] = gos[head].reshape(TOK, DIM).T
    delta = jnp.sum(go_cols[...].astype(F32) * rounded.astype(F32), axis=0, keepdims=True)

    beside = [lax.rem(y + step, NY) for step in range(1, NY)]
    virtual = [NY + yy for yy in beside]
    rest = [y, 2 * NY, own_slot]

    def both_cores(which, slot):
        return parts[which, slot, co].astype(F32) + from_core[which, slot].astype(F32)

    def home(which, number, sem, ctx, first_step):
        for step in range(first_step, N_HEAD):
            to = lax.rem(h + step, N_HEAD)
            push(sums.at[which, number, cols(to, PART), :], from_x.at[which, number, h], sem, ctx, to)

    def beside_home(which):
        for step, slot in enumerate(beside):
            y_sum[which, step] = both_cores(which, slot).astype(BF16)
            push(y_sum.at[which, step], from_y.at[which, step], YP + which, ctx_at(z, y + step + 1), h)

    def virtual_home(which):
        for step, slot in enumerate(virtual):
            sums[which, PLANES + step] = both_cores(which, slot).astype(BF16)
            plane = jnp.where(beside[step] <= y, z, z + 2)
            home(which, PLANES + step, XPV + which, ctx_at(plane, beside[step]), 0)

    def rest_home(which):
        sums[which, 0] = both_cores(which, 2 * NY).astype(BF16)
        home(which, 0, XP + 3 * which, ctx_at(z + 2, y), 0)
        sums[which, 2] = both_cores(which, own_slot).astype(BF16)
        home(which, 2, XP + 3 * which + 2, c, 1)
        from_x[which, 2, h] = sums[which, 2, cols(h, PART), :]

    def before_home(which):
        drain(from_y.at[0], recv.at[YP + which])
        before = both_cores(which, y)
        for step in range(NY - 1):
            before = before + from_y[which, step].astype(F32)
        sums[which, 1] = before.astype(BF16)
        home(which, 1, XP + 3 * which + 1, ctx_at(z + 3, y), 0)

    def value_group(slots, sem):
        for slot in slots:
            weights = (probs[slot] * inverse).astype(BF16)
            part = jnp.dot(weights, gos[...].reshape(ROWS, DIM), preferred_element_type=F32)
            parts[1, slot] = part.astype(BF16).reshape(NCORE, TOK, DIM)
        for slot in slots:
            push(parts.at[1, slot, 1 - co], from_core.at[1, slot], sem, sib, h)

    def key_group(slots, sem, query_grad):
        for slot in slots:
            keys, values = kv[0, slot].reshape(PAIR, DIM), kv[1, slot].reshape(PAIR, DIM)
            pushed = jnp.dot(values, go_cols[...], preferred_element_type=F32)
            slopes = (probs[slot] * inverse * (pushed - delta)).astype(BF16)
            part = jnp.dot(slopes, q_rows[...], preferred_element_type=F32) * SCALE
            parts[0, slot] = part.astype(BF16).reshape(NCORE, TOK, DIM)
            query_grad = query_grad + jnp.dot(keys.T, slopes, preferred_element_type=F32)
        for slot in slots:
            push(parts.at[0, slot, 1 - co], from_core.at[0, slot], sem, sib, h)
        return query_grad

    def drain_core(sem):
        drain(from_core.at[0, pl.ds(0, 3)], recv.at[sem])

    value_group(beside, CP)
    value_group(virtual, CP + 1)
    value_group(rest, CP + 2)
    query_grad = jnp.zeros((DIM, ROWS), F32)
    query_grad = key_group(beside, CP + 3, query_grad)
    drain_core(CP)
    beside_home(1)
    drain_core(CP + 1)
    virtual_home(1)
    drain_core(CP + 2)
    rest_home(1)
    query_grad = key_group(virtual, CP + 4, query_grad)
    drain_core(CP + 3)
    beside_home(0)
    query_grad = key_group(rest, CP + 5, query_grad)
    drain_core(CP + 4)
    virtual_home(0)

    query_grad = (query_grad * SCALE).astype(BF16)
    for head in range(GROUP):
        dq_rows[:, head * DIM : (head + 1) * DIM] = query_grad[:, head * TOK : (head + 1) * TOK].T
    for step in range(1, N_HEAD):
        to = lax.rem(h + step, N_HEAD)
        push(dq_rows.at[cols(to, PART), :], gq.at[:, cols(h, COLS)], DQ, c, to)
    own_dq = pltpu.make_async_copy(dq_rows.at[cols(h, PART), :], gq.at[:, cols(h, COLS)], local.at[LDQ])
    own_dq.start()

    drain(acol.at[pl.ds(0, 62)], recv.at[A1])

    def arrange_out(number, carry):
        aperm[2 * number] = acol[owned[0, number]]
        aperm[2 * number + 1] = acol[owned[1, number]]
        return carry

    lax.fori_loop(0, N_CTX, arrange_out, 0, unroll=4)

    def deliver_out(step, carry):
        to = lax.rem(c + step, N_CTX)
        push(
            aperm.at[pl.ds(2 * to, 2)], ao.at[:, pl.ds(tile_row, 16), cols(tile_head, DIM)], A2, to, h
        )
        return carry

    lax.fori_loop(1, N_CTX, deliver_out, 0)
    own_out = pltpu.make_async_copy(
        aperm.at[pl.ds(2 * c, 2)], ao.at[:, pl.ds(tile_row, 16), cols(tile_head, DIM)], local.at[LA]
    )
    own_out.start()
    drain_core(CP + 5)
    rest_home(0)
    before_home(1)
    before_home(0)

    for which in (1, 0):
        drain(from_x.at[0, pl.ds(PLANES, 3)], recv.at[XPV + which])
        drain(from_x.at[0, 0], recv.at[XP + 3 * which])
        drain(from_x.at[0, 0, pl.ds(0, 3)], recv.at[XP + 3 * which + 2])
        drain(from_x.at[0, 0], recv.at[XP + 3 * which + 1])
        for head in range(N_HEAD):
            piece = from_x[which, 0, head].astype(F32)
            for number in range(1, PLANES + NY - 1):
                piece = piece + from_x[which, number, head].astype(F32)
            grads[which, :, head * DIM : (head + 1) * DIM] = piece.astype(BF16)
    own_dk = pltpu.make_async_copy(grads.at[0], gk, local.at[LDK])
    own_dv = pltpu.make_async_copy(grads.at[1], gv, local.at[LDV])
    own_dk.start()
    own_dv.start()

    three_cols = pl.ds(0, 3 * COLS)
    drain(gperm.at[pl.ds(0, 62)], recv.at[A2])
    drain(gq.at[:, three_cols], recv.at[DQ])
    for copy in (own_out, own_dq, own_dk, own_dv):
        copy.wait()
    for sem in (G1, G2, A1, A2):
        drain(gperm.at[pl.ds(0, 62)], send.at[sem])
    for sem in (XQ, DQ):
        drain(gq.at[:, three_cols], send.at[sem])
    for which in range(2):
        for sem in (X0 + which, XP + 3 * which + 2):
            drain(from_x.at[0, 0, pl.ds(0, 3)], send.at[sem])
        for sem in (X1 + which, X2 + which, XP + 3 * which, XP + 3 * which + 1):
            drain(from_x.at[0, 0], send.at[sem])
        for sem in (Y1, YV, YP, XPV):
            drain(from_y.at[0], send.at[sem + which])
        for sem in range(3):
            drain(from_y.at[0], send.at[CP + 3 * which + sem])
        drain(kv.at[0, pl.ds(0, NY), 0], send.at[C1 + which])
        drain(kv.at[0, pl.ds(0, NY + 1), 0], send.at[CV + which])


def finish_body(ao, gq, gk, gv, ao_out, gq_out, gk_out, gv_out, sems):
    copies = [
        pltpu.make_async_copy(src, dst, sems.at[number])
        for number, (src, dst) in enumerate(((ao, ao_out), (gq, gq_out), (gk, gk_out), (gv, gv_out)))
    ]
    for copy in copies:
        copy.start()
    for copy in copies:
        copy.wait()


def finish(*arrays):
    anywhere = pl.BlockSpec(memory_space=pltpu.VMEM)
    hbm = pl.BlockSpec(memory_space=pltpu.HBM)
    return pl.pallas_call(
        finish_body,
        out_shape=tuple(jax.ShapeDtypeStruct(array.shape, array.dtype) for array in arrays),
        in_specs=[anywhere] * 4,
        out_specs=(hbm,) * 4,
        scratch_shapes=[pltpu.SemaphoreType.DMA((4,))],
        name="write_outputs",
    )(*arrays)


def shards(queries, keys, values, grad_out, owner_lists, doc_lengths):
    hbm = pl.BlockSpec(memory_space=pltpu.HBM)
    smem = pl.BlockSpec(memory_space=pltpu.SMEM)
    block = (TOK, DIM)
    ao, gq, gk, gv = pl.pallas_call(
        body,
        out_shape=(
            jax.ShapeDtypeStruct((2, TOK // 2, COLS), BF16),
            jax.ShapeDtypeStruct((PART, N_HEAD * COLS), BF16),
            jax.ShapeDtypeStruct((PART, N_HEAD * DIM), BF16),
            jax.ShapeDtypeStruct((PART, N_HEAD * DIM), BF16),
        ),
        in_specs=[hbm] * 4 + [smem] * 2,
        out_specs=(hbm,) * 4,
        scratch_shapes=[
            pltpu.VMEM((2, PART, N_HEAD * DIM), BF16),
            pltpu.VMEM((2, SLOTS, NCORE) + block, BF16),
            pltpu.VMEM((TOK, COLS), BF16),
            pltpu.VMEM((2 * N_CTX, 16, DIM), BF16),
            pltpu.VMEM((2 * N_CTX, 16, DIM), BF16),
            pltpu.VMEM((GROUP, 2, TOK // 2, DIM), BF16),
            pltpu.VMEM((2 * N_CTX, 16, DIM), BF16),
            pltpu.VMEM((2 * N_CTX, 16, DIM), BF16),
            pltpu.VMEM((GROUP, 2, TOK // 2, DIM), BF16),
            pltpu.VMEM((TOK, COLS), BF16),
            pltpu.VMEM((ROWS, DIM), BF16),
            pltpu.VMEM((DIM, ROWS), BF16),
            pltpu.VMEM((DIM, ROWS), BF16),
            pltpu.VMEM((SLOTS, PAIR, ROWS), F32),
            pltpu.VMEM((SLOTS, PAIR, ROWS), BF16),
            pltpu.VMEM((2, SLOTS, NCORE) + block, BF16),
            pltpu.VMEM((2, SLOTS) + block, BF16),
            pltpu.VMEM((2, NY - 1) + block, BF16),
            pltpu.VMEM((2, NY - 1) + block, BF16),
            pltpu.VMEM((2, PLANES + NY - 1) + block, BF16),
            pltpu.VMEM((2, PLANES + NY - 1, N_HEAD, PART, DIM), BF16),
            pltpu.VMEM((2, PART, N_HEAD * DIM), BF16),
            pltpu.VMEM((8, DIM), jnp.int32),
            pltpu.SMEM((8, DIM), jnp.int32),
            pltpu.SemaphoreType.DMA((N_SEM,)),
            pltpu.SemaphoreType.DMA((N_SEM,)),
            pltpu.SemaphoreType.DMA((N_LOCAL,)),
        ],
        compiler_params=pltpu.CompilerParams(
            collective_id=0, has_side_effects=True, vmem_limit_bytes=56 * 1024 * 1024
        ),
        cost_estimate=pl.CostEstimate(flops=4_000_000_000, bytes_accessed=4_000_000, transcendentals=2_300_000),
        name="attention_core",
    )(queries, keys, values, grad_out.reshape(2, TOK // 2, COLS), owner_lists.T, doc_lengths)
    return finish(ao.reshape(TOK, COLS), gq, gk, gv)


def solution(mesh):
    placed = (
        P(("ctx", "head"), None),
        P(("ctx", "head"), None),
        P(("ctx", "head"), None),
        P("ctx", "head"),
        P(),
        P(),
    )
    return jax.shard_map(
        shards,
        mesh=mesh,
        in_specs=placed,
        out_specs=(
            P("ctx", "head"),
            P(("ctx", "head"), None),
            P(("ctx", "head"), None),
            P(("ctx", "head"), None),
        ),
        check_vma=False,
    )
```

time: 48.8 us -> 47.3 us (0.969)
  Pallas kernels: 48 us -> 46.5 us
    pallas_call x1, Pallas kernels: 46.1 us -> 44.6 us  [shards(): pl.pallas_call(body, out_shape=(jax.ShapeDtypeStruct((2, TOK // 2, COLS),...]
where the time goes in v3:
time: 47.3 us; the launch traced here: 47.1 us
  Pallas kernels  46.5 us (98%)
  between operations  0.64 us (1%)
    pallas_call x1, Pallas kernels, shards(): pl.pallas_call(body, out_shape=(jax.ShapeDtypeStruct((2, TOK // 2, COLS),...  44.6 us
    pallas_call x1, Pallas kernels, finish(): pl.pallas_call(finish_body, out_shape=tuple((jax.ShapeDtypeStruct(array.s...  1.87 us

profile of v3, /device:TPU:1, one launch (start us, length us, event | category | flops | bytes accessed | tf_op | source)
XLA Modules:
  0.0 47.1 jit_solution(3985114175717576426)
XLA Ops:
  0.6 44.6 %attention_core.1 = (bf16[2,64,1024]{2,1,0:T(8,128)(2,1)}, bf16[32,4096]{1,0:T(8,128)(2,1)}, bf16[32,512]{1,0:T(8,128)(2,1)}, bf16[32,512]{1,0:T(8,128)(2,1)}) custom-call(bf16[32,4096]{1,0:T(8,128)(2,1)} %q_in.1, bf16[32,512]{1,0:T(8,128)(2,1)} %k_in.1, bf16[32,512]{1,0:T(8,128)(2,1)} %v_in.1, bf16[2,64,1024]{2,1,0:T(8,128)(2,1)} %bitcast.4, ...), custom_call_target="tpu_custom_call" | custom-call | flops 4000000000 | bytes 4000000 | tf_op jit(solution)/shard_map/attention_core/pallas_call | solution.py:447
  45.3 1.9 %write_outputs.1 = (bf16[128,1024]{1,0:T(8,128)(2,1)}, bf16[32,4096]{1,0:T(8,128)(2,1)}, bf16[32,512]{1,0:T(8,128)(2,1)}, bf16[32,512]{1,0:T(8,128)(2,1)}) custom-call(bf16[128,1024]{1,0:T(8,128)(2,1)} %bitcast.3, bf16[32,4096]{1,0:T(8,128)(2,1)} %get-tuple-element.9.gq, bf16[32,512]{1,0:T(8,128)(2,1)} %get-tuple-element.10.gk, ...), custom_call_target="tpu_custom_call" | custom-call | tf_op jit(solution)/shard_map/write_outputs/pallas_call | solution.py:433

commit v4 on v3

--- a/solution.py
+++ b/solution.py
@@ -97,9 +97,6 @@
 
     for ahead in range(NZ):
         greet_heads(ctx_at(z + ahead, y))
-    for step in range(1, NY):
-        greet_heads(ctx_at(z, y + step))
-        greet_heads(ctx_at(z + 2, y + step))
 
     lanes = lax.broadcasted_iota(jnp.int32, (8, DIM), 1)
     found = jnp.zeros((8, DIM), jnp.int32)
@@ -112,7 +109,7 @@
     for copy in local_copies[:4]:
         copy.wait()
     slot_copy.wait()
-    pl.semaphore_wait(barrier, N_CTX - 1 + (NZ + 2 * (NY - 1)) * (N_HEAD - 1))
+    pl.semaphore_wait(barrier, N_CTX - 1 + NZ * (N_HEAD - 1))
 
     def tile_of(number):
         return pl.multiple_of(16 * (number // GROUP), 16), lax.rem(number, GROUP)
@@ -123,7 +120,6 @@
         push(go_in.at[:, pl.ds(row, 16), cols(head, DIM)], gcol.at[pl.ds(2 * c, 2)], G1, to, h)
         return carry
 
-    lax.fori_loop(1, N_CTX, collect_grad, 0)
 
     def by_head(which, slot, sem, ctx, first_step):
         for step in range(first_step, N_HEAD):
@@ -133,23 +129,26 @@
             )
 
     def first_hop(which):
+        by_head(which, own_slot, X0, c, 1)
         by_head(which, y, X1, ctx_at(z + 1, y), 0)
         by_head(which, 2 * NY, X2, ctx_at(z + 2, y), 0)
-        by_head(which, own_slot, X0, c, 1)
-        for step in range(1, NY):
-            yy = lax.rem(y + step, NY)
-
-            @pl.when(yy > y)
-            def _():
-                by_head(which, own_slot, YV, ctx_at(z, yy), 0)
 
     first_hop(0)
+    first_hop(1)
+    lax.fori_loop(1, N_CTX, collect_grad, 0)
     for step in range(1, N_HEAD):
         to = lax.rem(h + step, N_HEAD)
         push(q_in.at[:, cols(to, COLS)], qs.at[cols(h, PART), :], XQ, c, to)
-    first_hop(1)
 
     def along_y(which):
+        drain(kv.at[0, 0, 0, pl.ds(0, 3 * PART), :], recv.at[X0 + which])
+        for step in range(1, NY):
+            yy = lax.rem(y + step, NY)
+
+            @pl.when(yy > y)
+            def _():
+                push(kv.at[which, own_slot, co], kv.at[which, own_slot, co], YV + which, ctx_at(z, yy), h)
+
         drain(kv.at[0, 0, 0], recv.at[X1 + which])
         for step in range(1, NY):
             push(kv.at[which, y, co], kv.at[which, y, co], Y1 + which, ctx_at(z, y + step), h)
@@ -200,7 +199,6 @@
     def to_other_core(which):
         drain(kv.at[0, pl.ds(0, 3), 0], recv.at[Y1 + which])
         push(kv.at[which, pl.ds(0, NY), co], kv.at[which, pl.ds(0, NY), co], C1 + which, sib, h)
-        drain(kv.at[0, 0, 0, pl.ds(0, 3 * PART), :], recv.at[X0 + which])
         drain(kv.at[0, pl.ds(0, 3), 0], recv.at[YV + which])
         push(kv.at[which, pl.ds(NY, NY + 1), co], kv.at[which, pl.ds(NY, NY + 1), co], CV + which, sib, h)
 

time: 47.3 us -> 45.5 us (0.962)
  Pallas kernels: 46.5 us -> 44.6 us
    pallas_call x1, Pallas kernels: 44.6 us -> 42.8 us  [shards(): pl.pallas_call(body, out_shape=(jax.ShapeDtypeStruct((2, TOK // 2, COLS),...]
where the time goes in v4:
time: 45.5 us; the launch traced here: 45.3 us
  Pallas kernels  44.6 us (98%)
  between operations  0.64 us (1%)
    pallas_call x1, Pallas kernels, shards(): pl.pallas_call(body, out_shape=(jax.ShapeDtypeStruct((2, TOK // 2, COLS),...  42.8 us
    pallas_call x1, Pallas kernels, finish(): pl.pallas_call(finish_body, out_shape=tuple((jax.ShapeDtypeStruct(array.s...  1.87 us

profile of v4, /device:TPU:1, one launch (start us, length us, event | category | flops | bytes accessed | tf_op | source)
XLA Modules:
  0.0 45.3 jit_solution(1227302291509044033)
XLA Ops:
  0.6 42.8 %attention_core.1 = (bf16[2,64,1024]{2,1,0:T(8,128)(2,1)}, bf16[32,4096]{1,0:T(8,128)(2,1)}, bf16[32,512]{1,0:T(8,128)(2,1)}, bf16[32,512]{1,0:T(8,128)(2,1)}) custom-call(bf16[32,4096]{1,0:T(8,128)(2,1)} %q_in.1, bf16[32,512]{1,0:T(8,128)(2,1)} %k_in.1, bf16[32,512]{1,0:T(8,128)(2,1)} %v_in.1, bf16[2,64,1024]{2,1,0:T(8,128)(2,1)} %bitcast.4, ...), custom_call_target="tpu_custom_call" | custom-call | flops 4000000000 | bytes 4000000 | tf_op jit(solution)/shard_map/attention_core/pallas_call | solution.py:445
  43.4 1.9 %write_outputs.1 = (bf16[128,1024]{1,0:T(8,128)(2,1)}, bf16[32,4096]{1,0:T(8,128)(2,1)}, bf16[32,512]{1,0:T(8,128)(2,1)}, bf16[32,512]{1,0:T(8,128)(2,1)}) custom-call(bf16[128,1024]{1,0:T(8,128)(2,1)} %bitcast.3, bf16[32,4096]{1,0:T(8,128)(2,1)} %get-tuple-element.9.gq, bf16[32,512]{1,0:T(8,128)(2,1)} %get-tuple-element.10.gk, ...), custom_call_target="tpu_custom_call" | custom-call | tf_op jit(solution)/shard_map/write_outputs/pallas_call | solution.py:431

commit v5 on v4

--- a/solution.py
+++ b/solution.py
@@ -32,15 +32,15 @@
 XQ, G1, G2, A1, A2, DQ = range(6)
 X0, X1, X2, Y1, YV, C1, CV, YP, XPV, XP, CP = (6, 8, 10, 12, 14, 16, 18, 20, 22, 24, 30)
 N_SEM = 36
-LK, LV, LRK, LRV, LQ, LG, LA, LDQ, LDK, LDV = range(10)
-N_LOCAL = 10
+LK, LV, LQ, LG, LS, LA = range(6)
+N_LOCAL = 6
 
 
 def body(
     q_in, k_in, v_in, go_in, owned, doc_lengths,
     ao, gq, gk, gv,
-    raw, kv, qs, gcol, gperm, gos, acol, aperm, out_rows, dq_rows,
-    q_rows, q_cols, go_cols, probs, rounded_probs, parts, from_core, y_sum, from_y, sums, from_x, grads,
+    kv, qs, gcol, gperm, gos, acol, aperm, out_rows, dq_rows,
+    q_rows, q_cols, go_cols, probs, rounded_probs, parts, from_core, y_sum, from_y, sums, from_x,
     slot_vec, slot_of, send, recv, local,
 ):
     c = lax.axis_index("ctx")
@@ -74,8 +74,6 @@
     local_copies = [
         pltpu.make_async_copy(k_in.at[:, cols(h, DIM)], kv.at[0, own_slot, co, cols(h, PART), :], local.at[LK]),
         pltpu.make_async_copy(v_in.at[:, cols(h, DIM)], kv.at[1, own_slot, co, cols(h, PART), :], local.at[LV]),
-        pltpu.make_async_copy(k_in, raw.at[0], local.at[LRK]),
-        pltpu.make_async_copy(v_in, raw.at[1], local.at[LRV]),
         pltpu.make_async_copy(q_in.at[:, cols(h, COLS)], qs.at[cols(h, PART), :], local.at[LQ]),
         pltpu.make_async_copy(
             go_in.at[:, pl.ds(tile_row, 16), cols(tile_head, DIM)], gcol.at[pl.ds(2 * c, 2)], local.at[LG]
@@ -98,17 +96,6 @@
     for ahead in range(NZ):
         greet_heads(ctx_at(z + ahead, y))
 
-    lanes = lax.broadcasted_iota(jnp.int32, (8, DIM), 1)
-    found = jnp.zeros((8, DIM), jnp.int32)
-    for number in range(2 * N_CTX):
-        found = jnp.where(lanes == owned[number % 2, number // 2], number, found)
-    slot_vec[...] = found
-    slot_copy = pltpu.make_async_copy(slot_vec, slot_of, local.at[LA])
-    slot_copy.start()
-
-    for copy in local_copies[:4]:
-        copy.wait()
-    slot_copy.wait()
     pl.semaphore_wait(barrier, N_CTX - 1 + NZ * (N_HEAD - 1))
 
     def tile_of(number):
@@ -125,7 +112,7 @@
         for step in range(first_step, N_HEAD):
             to = lax.rem(h + step, N_HEAD)
             push(
-                raw.at[which, :, cols(to, DIM)], kv.at[which, slot, co, cols(h, PART), :], sem + which, ctx, to
+                (k_in, v_in)[which].at[:, cols(to, DIM)], kv.at[which, slot, co, cols(h, PART), :], sem + which, ctx, to
             )
 
     def first_hop(which):
@@ -160,7 +147,17 @@
             def _():
                 push(kv.at[which, 2 * NY, co], kv.at[which, own_slot, co], YV + which, ctx_at(z, yy), h)
 
+    lanes = lax.broadcasted_iota(jnp.int32, (8, DIM), 1)
+    found = jnp.zeros((8, DIM), jnp.int32)
+    for number in range(2 * N_CTX):
+        found = jnp.where(lanes == owned[number % 2, number // 2], number, found)
+    slot_vec[...] = found
+    slot_copy = pltpu.make_async_copy(slot_vec, slot_of, local.at[LS])
+    slot_copy.start()
+
+    local_copies[0].wait()
     along_y(0)
+    local_copies[1].wait()
     along_y(1)
 
     q_pos = c * TOK + lax.broadcasted_iota(jnp.int32, (1, TOK), 1)
@@ -170,7 +167,8 @@
         first = jnp.where(q_pos >= begin, jnp.maximum(first, begin), first)
         begin = begin + doc_lengths[doc]
 
-    local_copies[5].wait()
+    local_copies[3].wait()
+    slot_copy.wait()
     drain(gcol.at[pl.ds(0, 62)], recv.at[G1])
 
     def arrange_grad(number, carry):
@@ -189,7 +187,7 @@
     lax.fori_loop(1, N_CTX, deliver_grad, 0)
     gos[tile_head, :, pl.ds(tile_row, 16), :] = gperm[pl.ds(2 * c, 2)]
 
-    local_copies[4].wait()
+    local_copies[2].wait()
     drain(qs.at[pl.ds(0, 3 * PART), :], recv.at[XQ])
     for head in range(GROUP):
         rows = qs[:, head * DIM : (head + 1) * DIM]
@@ -348,8 +346,7 @@
     for step in range(1, N_HEAD):
         to = lax.rem(h + step, N_HEAD)
         push(dq_rows.at[cols(to, PART), :], gq.at[:, cols(h, COLS)], DQ, c, to)
-    own_dq = pltpu.make_async_copy(dq_rows.at[cols(h, PART), :], gq.at[:, cols(h, COLS)], local.at[LDQ])
-    own_dq.start()
+    gq[:, cols(h, COLS)] = dq_rows[cols(h, PART), :]
 
     drain(acol.at[pl.ds(0, 62)], recv.at[A1])
 
@@ -386,17 +383,11 @@
             piece = from_x[which, 0, head].astype(F32)
             for number in range(1, PLANES + NY - 1):
                 piece = piece + from_x[which, number, head].astype(F32)
-            grads[which, :, head * DIM : (head + 1) * DIM] = piece.astype(BF16)
-    own_dk = pltpu.make_async_copy(grads.at[0], gk, local.at[LDK])
-    own_dv = pltpu.make_async_copy(grads.at[1], gv, local.at[LDV])
-    own_dk.start()
-    own_dv.start()
-
+            (gk, gv)[which][:, head * DIM : (head + 1) * DIM] = piece.astype(BF16)
     three_cols = pl.ds(0, 3 * COLS)
     drain(gperm.at[pl.ds(0, 62)], recv.at[A2])
     drain(gq.at[:, three_cols], recv.at[DQ])
-    for copy in (own_out, own_dq, own_dk, own_dv):
-        copy.wait()
+    own_out.wait()
     for sem in (G1, G2, A1, A2):
         drain(gperm.at[pl.ds(0, 62)], send.at[sem])
     for sem in (XQ, DQ):
@@ -427,6 +418,7 @@
 
 def finish(*arrays):
     anywhere = pl.BlockSpec(memory_space=pltpu.VMEM)
+    arrays = [pltpu.with_memory_space_constraint(array, pltpu.VMEM) for array in arrays]
     hbm = pl.BlockSpec(memory_space=pltpu.HBM)
     return pl.pallas_call(
         finish_body,
@@ -445,15 +437,14 @@
     ao, gq, gk, gv = pl.pallas_call(
         body,
         out_shape=(
-            jax.ShapeDtypeStruct((2, TOK // 2, COLS), BF16),
-            jax.ShapeDtypeStruct((PART, N_HEAD * COLS), BF16),
-            jax.ShapeDtypeStruct((PART, N_HEAD * DIM), BF16),
-            jax.ShapeDtypeStruct((PART, N_HEAD * DIM), BF16),
+            pltpu.VMEM((2, TOK // 2, COLS), BF16),
+            pltpu.VMEM((PART, N_HEAD * COLS), BF16),
+            pltpu.VMEM((PART, N_HEAD * DIM), BF16),
+            pltpu.VMEM((PART, N_HEAD * DIM), BF16),
         ),
         in_specs=[hbm] * 4 + [smem] * 2,
-        out_specs=(hbm,) * 4,
+        out_specs=(pl.BlockSpec(memory_space=pltpu.VMEM),) * 4,
         scratch_shapes=[
-            pltpu.VMEM((2, PART, N_HEAD * DIM), BF16),
             pltpu.VMEM((2, SLOTS, NCORE) + block, BF16),
             pltpu.VMEM((TOK, COLS), BF16),
             pltpu.VMEM((2 * N_CTX, 16, DIM), BF16),
@@ -474,7 +465,6 @@
             pltpu.VMEM((2, NY - 1) + block, BF16),
             pltpu.VMEM((2, PLANES + NY - 1) + block, BF16),
             pltpu.VMEM((2, PLANES + NY - 1, N_HEAD, PART, DIM), BF16),
-            pltpu.VMEM((2, PART, N_HEAD * DIM), BF16),
             pltpu.VMEM((8, DIM), jnp.int32),
             pltpu.SMEM((8, DIM), jnp.int32),
             pltpu.SemaphoreType.DMA((N_SEM,)),

time: 45.5 us -> 43.8 us (0.963)
  Pallas kernels: 44.6 us -> 42.8 us
    pallas_call x1, Pallas kernels: 1.87 us -> 0.84 us  [finish(): pl.pallas_call(finish_body, out_shape=tuple((jax.ShapeDtypeStruct(array.s...]
    pallas_call x1, Pallas kernels: 42.8 us -> 42 us  [shards(): pl.pallas_call(body, out_shape=(pltpu.VMEM((2, TOK // 2, COLS), BF16), pl...]
where the time goes in v5:
time: 43.8 us; the launch traced here: 43.4 us
  Pallas kernels  42.8 us (98%)
  between operations  0.64 us (1%)
    pallas_call x1, Pallas kernels, shards(): pl.pallas_call(body, out_shape=(pltpu.VMEM((2, TOK // 2, COLS), BF16), pl...  42 us

profile of v5, /device:TPU:1, one launch (start us, length us, event | category | flops | bytes accessed | tf_op | source)
XLA Modules:
  0.0 43.4 jit_solution(13362352878269021844)
XLA Ops:
  0.6 42.0 %attention_core.1 = (bf16[2,64,1024]{2,1,0:T(8,128)(2,1)S(1)}, bf16[32,4096]{1,0:T(8,128)(2,1)S(1)}, bf16[32,512]{1,0:T(8,128)(2,1)S(1)}, bf16[32,512]{1,0:T(8,128)(2,1)S(1)}) custom-call(bf16[32,4096]{1,0:T(8,128)(2,1)} %q_in.1, bf16[32,512]{1,0:T(8,128)(2,1)} %k_in.1, bf16[32,512]{1,0:T(8,128)(2,1)} %v_in.1, bf16[2,64,1024]{2,1,0:T(8,128)(2,1)} %bitcast.4, ...), custom_call_target="tpu_custom_call" | custom-call | flops 4000000000 | bytes 4000000 | tf_op jit(solution)/shard_map/attention_core/pallas_call | solution.py:437
  42.6 0.8 %write_outputs.1 = (bf16[128,1024]{1,0:T(8,128)(2,1)}, bf16[32,4096]{1,0:T(8,128)(2,1)}, bf16[32,512]{1,0:T(8,128)(2,1)}, bf16[32,512]{1,0:T(8,128)(2,1)}) custom-call(bf16[128,1024]{1,0:T(8,128)(2,1)S(1)} %bitcast.3, bf16[32,4096]{1,0:T(8,128)(2,1)S(1)} %get-tuple-element.9.gq, bf16[32,512]{1,0:T(8,128)(2,1)S(1)} %get-tuple-element.10.gk, ...), custom_call_target="tpu_custom_call" | custom-call | tf_op jit(solution)/shard_map/write_outputs/pallas_call | solution.py:423

commit v6 on v5

--- a/solution.py
+++ b/solution.py
@@ -121,11 +121,11 @@
         by_head(which, 2 * NY, X2, ctx_at(z + 2, y), 0)
 
     first_hop(0)
-    first_hop(1)
-    lax.fori_loop(1, N_CTX, collect_grad, 0)
     for step in range(1, N_HEAD):
         to = lax.rem(h + step, N_HEAD)
         push(q_in.at[:, cols(to, COLS)], qs.at[cols(h, PART), :], XQ, c, to)
+    first_hop(1)
+    lax.fori_loop(1, N_CTX, collect_grad, 0)
 
     def along_y(which):
         drain(kv.at[0, 0, 0, pl.ds(0, 3 * PART), :], recv.at[X0 + which])

time: 43.8 us -> 43.5 us (level)
  no operation moved by 1% of the time
where the time goes in v6:
time: 43.5 us; the launch traced here: 43.4 us
  Pallas kernels  42.7 us (98%)
  between operations  0.64 us (1%)
    pallas_call x1, Pallas kernels, shards(): pl.pallas_call(body, out_shape=(pltpu.VMEM((2, TOK // 2, COLS), BF16), pl...  41.9 us

profile of v6, /device:TPU:1, one launch (start us, length us, event | category | flops | bytes accessed | tf_op | source)
XLA Modules:
  0.0 43.4 jit_solution(434381086549665953)
XLA Ops:
  0.6 41.9 %attention_core.1 = (bf16[2,64,1024]{2,1,0:T(8,128)(2,1)S(1)}, bf16[32,4096]{1,0:T(8,128)(2,1)S(1)}, bf16[32,512]{1,0:T(8,128)(2,1)S(1)}, bf16[32,512]{1,0:T(8,128)(2,1)S(1)}) custom-call(bf16[32,4096]{1,0:T(8,128)(2,1)} %q_in.1, bf16[32,512]{1,0:T(8,128)(2,1)} %k_in.1, bf16[32,512]{1,0:T(8,128)(2,1)} %v_in.1, bf16[2,64,1024]{2,1,0:T(8,128)(2,1)} %bitcast.4, ...), custom_call_target="tpu_custom_call" | custom-call | flops 4000000000 | bytes 4000000 | tf_op jit(solution)/shard_map/attention_core/pallas_call | solution.py:437
  42.6 0.8 %write_outputs.1 = (bf16[128,1024]{1,0:T(8,128)(2,1)}, bf16[32,4096]{1,0:T(8,128)(2,1)}, bf16[32,512]{1,0:T(8,128)(2,1)}, bf16[32,512]{1,0:T(8,128)(2,1)}) custom-call(bf16[128,1024]{1,0:T(8,128)(2,1)S(1)} %bitcast.3, bf16[32,4096]{1,0:T(8,128)(2,1)S(1)} %get-tuple-element.9.gq, bf16[32,512]{1,0:T(8,128)(2,1)S(1)} %get-tuple-element.10.gk, ...), custom_call_target="tpu_custom_call" | custom-call | tf_op jit(solution)/shard_map/write_outputs/pallas_call | solution.py:423

commit v7 on v6

--- a/solution.py
+++ b/solution.py
@@ -348,6 +348,8 @@
         push(dq_rows.at[cols(to, PART), :], gq.at[:, cols(h, COLS)], DQ, c, to)
     gq[:, cols(h, COLS)] = dq_rows[cols(h, PART), :]
 
+    drain_core(CP + 5)
+    rest_home(0)
     drain(acol.at[pl.ds(0, 62)], recv.at[A1])
 
     def arrange_out(number, carry):
@@ -369,8 +371,6 @@
         aperm.at[pl.ds(2 * c, 2)], ao.at[:, pl.ds(tile_row, 16), cols(tile_head, DIM)], local.at[LA]
     )
     own_out.start()
-    drain_core(CP + 5)
-    rest_home(0)
     before_home(1)
     before_home(0)
 

time: 43.5 us -> 44.1 us (1.014)
  Pallas kernels: 42.7 us -> 43.3 us
    pallas_call x1, Pallas kernels: 41.9 us -> 42.5 us  [shards(): pl.pallas_call(body, out_shape=(pltpu.VMEM((2, TOK // 2, COLS), BF16), pl...]
where the time goes in v7:
time: 44.1 us; the launch traced here: 44 us
  Pallas kernels  43.3 us (98%)
  between operations  0.64 us (1%)
    pallas_call x1, Pallas kernels, shards(): pl.pallas_call(body, out_shape=(pltpu.VMEM((2, TOK // 2, COLS), BF16), pl...  42.5 us

profile of v7, /device:TPU:1, one launch (start us, length us, event | category | flops | bytes accessed | tf_op | source)
XLA Modules:
  0.0 44.0 jit_solution(1382454191076628807)
XLA Ops:
  0.6 42.5 %attention_core.1 = (bf16[2,64,1024]{2,1,0:T(8,128)(2,1)S(1)}, bf16[32,4096]{1,0:T(8,128)(2,1)S(1)}, bf16[32,512]{1,0:T(8,128)(2,1)S(1)}, bf16[32,512]{1,0:T(8,128)(2,1)S(1)}) custom-call(bf16[32,4096]{1,0:T(8,128)(2,1)} %q_in.1, bf16[32,512]{1,0:T(8,128)(2,1)} %k_in.1, bf16[32,512]{1,0:T(8,128)(2,1)} %v_in.1, bf16[2,64,1024]{2,1,0:T(8,128)(2,1)} %bitcast.4, ...), custom_call_target="tpu_custom_call" | custom-call | flops 4000000000 | bytes 4000000 | tf_op jit(solution)/shard_map/attention_core/pallas_call | solution.py:437
  43.1 0.8 %write_outputs.1 = (bf16[128,1024]{1,0:T(8,128)(2,1)}, bf16[32,4096]{1,0:T(8,128)(2,1)}, bf16[32,512]{1,0:T(8,128)(2,1)}, bf16[32,512]{1,0:T(8,128)(2,1)}) custom-call(bf16[128,1024]{1,0:T(8,128)(2,1)S(1)} %bitcast.3, bf16[32,4096]{1,0:T(8,128)(2,1)S(1)} %get-tuple-element.9.gq, bf16[32,512]{1,0:T(8,128)(2,1)S(1)} %get-tuple-element.10.gk, ...), custom_call_target="tpu_custom_call" | custom-call | tf_op jit(solution)/shard_map/write_outputs/pallas_call | solution.py:423
